TPU v7x, 128 devices: a whole 4x4x4 slice. The times are simulated.
128 devices in a mesh: dp: 4 (over x), block: 32 (over z, y, core).
Axes of the slice: x: 4, y: 4, z: 4, core: 2. Of those that a mesh axis runs over, the one named last changes fastest.
Arguments:
- grad: float32 [1024, 28672], P(('dp', 'block')), may hold values from -6 to 6
- factors: float32 [4, 32, 1024, 1024], P('dp', 'block'), as said below
- owners: int32 [28], replicated, may hold values from 0 to 31, as said below
Outputs:
- new_factors: float32 [4, 32, 1024, 1024], P('dp', 'block')
- update: float32 [1024, 28672], P(('dp', 'block'))
Inputs may be any that keep to these rules, and one draw needn't show every extreme that they name: `owners`: no owner is named more than 2 times, and some owner exactly 2 times. `factors`: every [1024, 1024] matrix is symmetric positive definite.
All inputs are finite; a program needn't handle non-finite values.
Results may differ from a plain program's by a relative error of at most 0.00013.
Values sent between devices are 32-bit elements; how exact they have to be, the bound alone decides.
No kernel may reach another device: no remote copies, remote signals or barrier semaphores. Data moves between devices by JAX's collectives and lax.ppermute only.
A program may use at most 128 MiB of HBM per device.

v0:
```python
import jax
import jax.numpy as jnp
from jax import lax
from jax.experimental import pallas as pl
from jax.experimental.pallas import tpu as pltpu
from jax.sharding import PartitionSpec as P

BOTH = ("dp", "block")
TILE = 256
VMEM_LIMIT = 56 * 1024 * 1024

decay_rate = 0.9
epsilon = 1e-06


def vmem():
    return pl.BlockSpec(memory_space=pltpu.VMEM)


def smem():
    return pl.BlockSpec(memory_space=pltpu.SMEM)


def diag_mask():
    rows = lax.broadcasted_iota(jnp.int32, (TILE, TILE), 0)
    cols = lax.broadcasted_iota(jnp.int32, (TILE, TILE), 1)
    return rows, cols


def span(index):
    return slice(index * TILE, (index + 1) * TILE)


def split(value):
    high = value.astype(jnp.bfloat16)
    low = (value - high.astype(jnp.float32)).astype(jnp.bfloat16)
    return high, low


def dot3(a_high, a_low, b_high, b_low):
    def one(a, b):
        return jnp.dot(a, b, preferred_element_type=jnp.float32)

    return one(a_high, b_high) + (one(a_high, b_low) + one(a_low, b_high))


def put_split(high_ref, low_ref, i, j, block):
    high, low = split(block)
    high_ref[span(i), span(j)] = high
    low_ref[span(i), span(j)] = low


def put_both(high_ref, low_ref, i, j, block):
    put_split(high_ref, low_ref, i, j, block)
    if i != j:
        put_split(high_ref, low_ref, j, i, block.T)


def deal_kernel(owners_ref, grad_ref, out_ref, count_ref):
    owner_count = count_ref.shape[0]
    col_blocks = owners_ref.shape[0]
    width = out_ref.shape[-1]

    @pl.loop(0, owner_count)
    def _(o):
        count_ref[o] = 0

    out_ref[...] = jnp.zeros_like(out_ref)

    @pl.loop(0, col_blocks)
    def _(c):
        owner = owners_ref[c]
        slot = count_ref[owner]
        count_ref[owner] = slot + 1
        cols = pl.ds(pl.multiple_of(c * width, width), width)
        out_ref[slot * owner_count + owner] = grad_ref[:, cols]


def deal(owners, grad, owner_count):
    rows = grad.shape[0]
    width = grad.shape[1] // owners.shape[0]
    return pl.pallas_call(
        deal_kernel,
        out_shape=jax.ShapeDtypeStruct((2 * owner_count, rows, width), jnp.float32),
        in_specs=[smem(), vmem()],
        out_specs=vmem(),
        scratch_shapes=[pltpu.SMEM((owner_count,), jnp.int32)],
        compiler_params=pltpu.CompilerParams(vmem_limit_bytes=VMEM_LIMIT),
        cost_estimate=pl.CostEstimate(flops=0, bytes_accessed=3 * 2**20, transcendentals=0),
        name="deal",
    )(owners, grad)


def collect_kernel(owners_ref, scale_ref, back_ref, out_ref, count_ref):
    owner_count = count_ref.shape[0]
    col_blocks = owners_ref.shape[0]
    width = back_ref.shape[-1]

    @pl.loop(0, owner_count)
    def _(o):
        count_ref[o] = 0

    @pl.loop(0, col_blocks)
    def _(c):
        owner = owners_ref[c]
        slot = count_ref[owner]
        count_ref[owner] = slot + 1
        place = slot * owner_count + owner
        cols = pl.ds(pl.multiple_of(c * width, width), width)
        out_ref[:, cols] = back_ref[place] * scale_ref[place]


def collect(owners, scales, back):
    places, rows, width = back.shape
    return pl.pallas_call(
        collect_kernel,
        out_shape=jax.ShapeDtypeStruct((rows, owners.shape[0] * width), jnp.float32),
        in_specs=[smem(), smem(), vmem()],
        out_specs=vmem(),
        scratch_shapes=[pltpu.SMEM((places // 2,), jnp.int32)],
        compiler_params=pltpu.CompilerParams(vmem_limit_bytes=VMEM_LIMIT),
        cost_estimate=pl.CostEstimate(flops=0, bytes_accessed=3 * 2**20, transcendentals=0),
        name="collect",
    )(owners, scales, back)


def lower_blocks(tiles):
    return [(i, j) for j in range(tiles) for i in range(j + 1, tiles)]


def root_kernel(a_ref, xh_ref, xl_ref, pack_ref, sh, sl, s2, s2h, s2l, s3h, s3l, qh, ql):
    size = a_ref.shape[0]
    tiles = size // TILE
    rows, cols = diag_mask()
    on_diag = rows == cols
    trace = jnp.float32(0.0)
    for b in range(tiles):
        trace += jnp.sum(jnp.where(on_diag, a_ref[span(b), span(b)], 0.0))
    shrink = 0.25 / (2.0 * trace / size)

    def step_block(i, j):
        block = a_ref[span(i), span(j)] * -shrink
        if i == j:
            block = jnp.where(on_diag, 1.25 + block, block)
        return block

    for i in range(tiles):
        for j in range(tiles):
            put_split(sh, sl, i, j, step_block(i, j))

    def product(ah, al, bh, bl, j):
        low_rows = slice(j * TILE, size)
        return dot3(ah[low_rows, :], al[low_rows, :], bh[:, span(j)], bl[:, span(j)])

    for j in range(tiles):
        column = product(sh, sl, sh, sl, j)
        s2[j * TILE :, span(j)] = column
        for i in range(j, tiles):
            put_both(s2h, s2l, i, j, column[span(i - j)])
    for j in range(tiles):
        column = product(sh, sl, s2h, s2l, j)
        for i in range(j, tiles):
            block = column[span(i - j)]
            put_both(s3h, s3l, i, j, block)
            put_both(qh, ql, i, j, block - 1.25 * s2[span(i), span(j)])
    for j in range(tiles):
        column = product(s3h, s3l, qh, ql, j)
        for i in range(j, tiles):
            block = column[span(i - j)] + 1.25 * step_block(i, j)
            put_both(xh_ref, xl_ref, i, j, block)
            if i != j:
                pack_ref[span(lower_blocks(tiles).index((i, j)))] = block
            else:
                s2[span(i), span(i)] = block
    offset = len(lower_blocks(tiles))
    last = (offset + tiles // 2) * TILE
    for pair in range(tiles // 2):
        first = s2[span(2 * pair), span(2 * pair)]
        second = s2[span(2 * pair + 1), span(2 * pair + 1)]
        pack_ref[span(offset + pair)] = jnp.where(rows >= cols, first, second)
        diagonal = jnp.sum(jnp.where(on_diag, second, 0.0), axis=0, keepdims=True)
        pack_ref[last + pair * 8 : last + pair * 8 + 8] = jnp.broadcast_to(diagonal, (8, TILE))


def packed_rows(size):
    tiles = size // TILE
    return (len(lower_blocks(tiles)) + tiles // 2) * TILE + 8 * (tiles // 2)


def root(factor):
    size = factor.shape[0]
    half = jax.ShapeDtypeStruct((size, size), jnp.bfloat16)
    return pl.pallas_call(
        root_kernel,
        out_shape=[half, half, jax.ShapeDtypeStruct((packed_rows(size), TILE), jnp.float32)],
        in_specs=[vmem()],
        out_specs=[vmem()] * 3,
        scratch_shapes=[pltpu.VMEM((size, size), jnp.bfloat16)] * 2
        + [pltpu.VMEM((size, size), jnp.float32)]
        + [pltpu.VMEM((size, size), jnp.bfloat16)] * 6,
        compiler_params=pltpu.CompilerParams(vmem_limit_bytes=VMEM_LIMIT),
        cost_estimate=pl.CostEstimate(
            flops=11 * size**3, bytes_accessed=10 * 2**20, transcendentals=0
        ),
        name="root",
    )(factor)


def unpack_block(pack_ref, tiles, i, j, rows, cols):
    if i != j:
        return pack_ref[span(lower_blocks(tiles).index((i, j)))]
    offset = len(lower_blocks(tiles))
    last = (offset + tiles // 2) * TILE
    both = pack_ref[span(offset + i // 2)]
    if i % 2 == 0:
        return jnp.where(rows >= cols, both, both.T)
    diagonal = pack_ref[last + (i // 2) * 8 : last + (i // 2) * 8 + 1]
    return jnp.where(rows == cols, diagonal, jnp.where(rows < cols, both, both.T))


def apply_kernel(
    place_ref, xh_ref, xl_ref, pack_ref, near_ref, far_ref, raw_ref, sums_ref,
    ph, pw, lh, ll, rh, rl, gh, gl, uh, ul,
):
    size = xh_ref.shape[0]
    half = size // 2
    tiles = size // TILE
    side = place_ref[0]
    rows, cols = diag_mask()

    for i in range(tiles):
        for j in range(i + 1):
            put_both(ph, pw, i, j, unpack_block(pack_ref, tiles, i, j, rows, cols))

    def place_left(high_ref, low_ref):
        for r in range(2):
            source_rows = pl.ds(pl.multiple_of(place_ref[1 + r] * TILE, TILE), TILE)
            for c in range(tiles):
                source_cols = pl.ds(pl.multiple_of(place_ref[1 + c] * TILE, TILE), TILE)
                lh[span(r), span(c)] = high_ref[source_rows, source_cols]
                ll[span(r), span(c)] = low_ref[source_rows, source_cols]

    @pl.when(side == 0)
    def _():
        place_left(xh_ref, xl_ref)
        rh[...] = ph[...]
        rl[...] = pw[...]

    @pl.when(side != 0)
    def _():
        place_left(ph, pw)
        rh[...] = xh_ref[...]
        rl[...] = xl_ref[...]

    total = jnp.zeros((8, TILE), jnp.float32)
    for part, ref in enumerate((near_ref, far_ref)):
        for r in range(half // TILE):
            for c in range(tiles):
                block = ref[span(r), span(c)]
                put_split(gh, gl, part * (half // TILE) + r, c, block)
                total += jnp.sum((block * block).reshape(TILE // 8, 8, TILE), axis=0)
    grad_sum = jnp.sum(total)
    for j in range(tiles):
        column = dot3(lh[...], ll[...], gh[:, span(j)], gl[:, span(j)])
        high, low = split(column)
        uh[:, span(j)] = high
        ul[:, span(j)] = low
    total = jnp.zeros((8, TILE), jnp.float32)
    for j in range(tiles):
        column = dot3(uh[...], ul[...], rh[:, span(j)], rl[:, span(j)])
        raw_ref[:, span(j)] = column
        total += jnp.sum((column * column).reshape(half // 8, 8, TILE), axis=0)
    raw_sum = jnp.sum(total)
    lane = lax.broadcasted_iota(jnp.int32, (8, 128), 1)
    sums_ref[...] = jnp.where(lane == 0, raw_sum, jnp.where(lane == 1, grad_sum, 0.0))


def apply_roots(place, x_high, x_low, pack, near, far):
    size = x_high.shape[0]
    half = size // 2
    big = pltpu.VMEM((size, size), jnp.bfloat16)
    small = pltpu.VMEM((half, size), jnp.bfloat16)
    return pl.pallas_call(
        apply_kernel,
        out_shape=[
            jax.ShapeDtypeStruct((half, size), jnp.float32),
            jax.ShapeDtypeStruct((8, 128), jnp.float32),
        ],
        in_specs=[smem()] + [vmem()] * 5,
        out_specs=[vmem()] * 2,
        scratch_shapes=[big, big, small, small, big, big, big, big, small, small],
        compiler_params=pltpu.CompilerParams(vmem_limit_bytes=VMEM_LIMIT),
        cost_estimate=pl.CostEstimate(
            flops=6 * size**3, bytes_accessed=12 * 2**20, transcendentals=0
        ),
        name="apply_roots",
    )(place, x_high, x_low, pack, near, far)


def per_device(grad, factors, owners):
    row_count = grad.shape[0]
    block_size = factors.shape[-1]
    owner_count = lax.axis_size("block")
    dp_index = lax.axis_index("dp")
    blk_index = lax.axis_index("block")
    side = dp_index % 2
    slot = dp_index // 2
    outer_pair = (dp_index == 0) | (dp_index == 3)
    groups = [[x * owner_count + b for x in pair for b in range(owner_count)] for pair in ((0, 3), (1, 2))]

    def exchange(x):
        return lax.all_to_all(
            x, BOTH, split_axis=0, concat_axis=0, tiled=True, axis_index_groups=groups
        )

    def swap(x):
        return lax.ppermute(x, "dp", [(i, i ^ 1) for i in range(4)])

    other_grad = swap(grad)
    near = exchange(deal(owners, grad, owner_count)).reshape(block_size // 2, block_size)
    own_factor = factors[0, 0]
    x_high, x_low, pack = root(own_factor)
    pack, other_grad = lax.optimization_barrier((pack, other_grad))
    other_pack = swap(pack)
    far = exchange(deal(owners, other_grad, owner_count)).reshape(block_size // 2, block_size)

    order = jnp.where(outer_pair, jnp.array([0, 3, 1, 2]), jnp.array([1, 2, 0, 3]))
    place = jnp.concatenate([side[None], order]).astype(jnp.int32)
    raw, sums = apply_roots(place, x_high, x_low, other_pack, near, far)
    back = exchange(raw.reshape(2 * owner_count, row_count, block_size))
    all_sums = lax.all_gather(sums[0], BOTH)
    raw_sums = all_sums[:, 0].reshape(2, 2, owner_count).sum(axis=1).reshape(-1)
    grad_sums = all_sums[:, 1].reshape(2, 2, owner_count)[:, 0].reshape(-1)
    count = block_size * block_size
    scales = jnp.sqrt(grad_sums / count + epsilon) / jnp.sqrt(raw_sums / count + epsilon)
    update = collect(owners, scales, back)

    quarter = block_size // 4
    block_grad = jnp.where(
        outer_pair,
        jnp.concatenate([near[:quarter], far, near[quarter:]]),
        jnp.concatenate([far[:quarter], near, far[quarter:]]),
    )
    flipped = jnp.where(side == 0, block_grad, block_grad.T)
    outer = lax.dot_general(
        flipped, flipped, (((1,), (1,)), ((), ())), precision=lax.Precision.HIGH
    )
    used = jnp.sum(owners == blk_index) > slot
    new_own = decay_rate * own_factor + jnp.where(
        used, (1.0 - decay_rate) / block_size * outer, 0.0
    )
    return (new_own[None, None], update)


def solution(mesh):
    placed = (P(BOTH, None), P("dp", "block", None, None), P())
    return jax.shard_map(
        per_device,
        mesh=mesh,
        in_specs=placed,
        out_specs=(P("dp", "block", None, None), P(BOTH, None)),
        check_vma=False,
    )
```

profile of v0, /device:TPU:1, one launch (start us, length us, event | category | flops | bytes accessed | tf_op | source)
XLA Modules:
  0.0 172.5 jit_solution(18409247713303364351)
XLA Ops:
  0.6 0.0 copy-start.3
  0.6 3.2 %deal.2 = f32[64,8,1024]{2,1,0:T(8,128)} custom-call(s32[28]{0:T(128)} %owners_ref.5, f32[8,28672]{1,0:T(8,128)} %grad_ref.1), custom_call_target="tpu_custom_call" | custom-call | bytes 3145728 | tf_op jit(solution)/shard_map/deal/pallas_call | solution.py:82
  3.9 12.2 %all-to-all-start = ((f32[64,8,1024]{2,1,0:T(8,128)}), f32[64,8,1024]{2,1,0:T(8,128)S(1)}, u32[]{:S(2)}, u32[]{:S(2)}) async-start(f32[64,8,1024]{2,1,0:T(8,128)} %deal.2), calls=%async_computation | async-start | bytes 4194304 | tf_op jit(solution)/shard_map/all_to_all | solution.py:312
  16.1 0.0 copy-done.3
  16.1 0.1 collective-permute-start
  16.2 17.7 %root.1 = (bf16[1024,1024]{1,0:T(8,128)(2,1)}, bf16[1024,1024]{1,0:T(8,128)(2,1)}, f32[2064,256]{1,0:T(8,128)}) custom-call(f32[1024,1024]{1,0:T(8,128)} %bitcast.26), custom_call_target="tpu_custom_call" | custom-call | flops 11811160064 | bytes 10485760 | tf_op jit(solution)/shard_map/root/pallas_call | solution.py:193
  33.9 0.0 copy-start.5
  33.9 0.0 copy-start.6
  33.9 0.0 copy-start.7
  33.9 3.7 %collective-permute-done.grad_ref = f32[8,28672]{1,0:T(8,128)S(1)} collective-permute-done((f32[8,28672]{1,0:T(8,128)S(1)}, f32[8,28672]{1,0:T(8,128)S(1)}, u32[]{:S(2)}, u32[]{:S(2)}) %collective-permute-start) | collective-permute-done | bytes 917536 | tf_op jit(solution)/shard_map/ppermute | solution.py:317
  37.6 0.0 copy-start.4
  37.6 0.1 collective-permute-start.1
  37.7 0.8 copy-done.4
  38.6 3.2 %deal.3 = f32[64,8,1024]{2,1,0:T(8,128)} custom-call(s32[28]{0:T(128)} %owners_ref.5, f32[8,28672]{1,0:T(8,128)} %copy-done.4), custom_call_target="tpu_custom_call" | custom-call | bytes 3145728 | tf_op jit(solution)/shard_map/deal/pallas_call | solution.py:82
  41.8 3.1 %all-to-all-done = f32[64,8,1024]{2,1,0:T(8,128)S(1)} async-done(((f32[64,8,1024]{2,1,0:T(8,128)}), f32[64,8,1024]{2,1,0:T(8,128)S(1)}, u32[]{:S(2)}, u32[]{:S(2)}) %all-to-all-start) | async-done | bytes 2097184 | tf_op jit(solution)/shard_map/all_to_all | solution.py:312
  44.9 0.0 copy-start
  44.9 8.2 %all-to-all-start.1 = ((f32[64,8,1024]{2,1,0:T(8,128)}), f32[64,8,1024]{2,1,0:T(8,128)}, u32[]{:S(2)}, u32[]{:S(2)}) async-start(f32[64,8,1024]{2,1,0:T(8,128)} %deal.3), calls=%async_computation.1 | async-start | bytes 4194304 | tf_op jit(solution)/shard_map/all_to_all | solution.py:312
  53.0 0.0 copy-done.5
  53.1 0.7 fusion.5
  54.4 0.0 copy-done.6
  54.4 0.0 copy-done.7
  54.5 0.6 pad_add_fusion.place_ref
  55.1 1.2 slice_bitcast_fusion.3
  56.2 0.0 copy-done
  56.2 25.5 %all-to-all-done.1 = f32[64,8,1024]{2,1,0:T(8,128)} async-done(((f32[64,8,1024]{2,1,0:T(8,128)}), f32[64,8,1024]{2,1,0:T(8,128)}, u32[]{:S(2)}, u32[]{:S(2)}) %all-to-all-start.1) | async-done | bytes 2097184 | tf_op jit(solution)/shard_map/all_to_all | solution.py:312
  81.7 2.4 %collective-permute-done.1.pack_ref = f32[2064,256]{1,0:T(8,128)} collective-permute-done((f32[2064,256]{1,0:T(8,128)}, f32[2064,256]{1,0:T(8,128)}, u32[]{:S(2)}, u32[]{:S(2)}) %collective-permute-start.1) | collective-permute-done | bytes 2113568 | tf_op jit(solution)/shard_map/ppermute | solution.py:317
  84.1 13.4 %apply_roots.1 = (f32[512,1024]{1,0:T(8,128)}, f32[8,128]{1,0:T(8,128)}) custom-call(s32[5]{0:T(128)} %pad_add_fusion.place_ref, bf16[1024,1024]{1,0:T(8,128)(2,1)} %get-tuple-element.11.xh_ref, bf16[1024,1024]{1,0:T(8,128)(2,1)} %get-tuple-element.12.xl_ref, f32[2064,256]{1,0:T(8,128)} %collective-permute-done.1.pack_ref, f32[512,1024]{1,0:T(8,128)} %bitcast.24, ...), custom_call_target="tpu_custom_call" | custom-call | flops 6442450944 | bytes 12582912 | tf_op jit(solution)/shard_map/apply_roots/pallas_call | solution.py:283
  97.5 0.0 copy-start.1
  97.5 12.4 %all-to-all-start.2 = ((f32[64,8,1024]{2,1,0:T(8,128)}), f32[64,8,1024]{2,1,0:T(8,128)}, u32[]{:S(2)}, u32[]{:S(2)}) async-start(f32[64,8,1024]{2,1,0:T(8,128)} %bitcast.27), calls=%async_computation.2 | async-start | bytes 4194304 | tf_op jit(solution)/shard_map/all_to_all | solution.py:312
  110.0 0.0 copy-start.2
  110.0 1.9 %slice_bitcast_fusion.1 = (f32[256,1024]{1,0:T(8,128)S(1)}, f32[256,1024]{1,0:T(8,128)S(1)}) fusion(f32[64,8,1024]{2,1,0:T(8,128)} %all-to-all-done.1), kind=kLoop, calls=%fused_computation.6 | loop fusion | bytes 4194304 | tf_op jit(solution)/shard_map/slice | solution.py:342
  111.8 0.0 copy-done.1
  111.8 0.0 copy-done.2
  111.9 3.7 %maximum_select_fusion = f32[1024,1024]{1,0:T(8,128)} fusion(f32[256,1024]{1,0:T(8,128)S(1)} %copy-done.2, f32[512,1024]{1,0:T(8,128)} %bitcast.2.far_ref, f32[256,1024]{1,0:T(8,128)S(1)} %get-tuple-element.20, f32[256,1024]{1,0:T(8,128)S(1)} %get-tuple-element.19, f32[512,1024]{1,0:T(8,128)S(1)} %bitcast.25, f32[256,1024]{1,0:T(8,128)S(1)} %get-tuple-element.18, ...), kind=kLoop, calls=%fused_computation | loop fusion | flops 5242880 | bytes 12582913 | tf_op jit(solution)/shard_map/jit(_where)/select_n | solution.py:339
  115.6 5.4 %copy.9 = f32[1024,1024]{0,1:T(8,128)} copy(f32[1024,1024]{1,0:T(8,128)} %maximum_select_fusion) | data formatting | bytes 8388608 | tf_op jit(solution)/shard_map/jit(_where)/select_n | solution.py:339
  120.9 15.4 %add_bitcast_fusion = f32[1,1,1024,1024]{3,2,1,0:T(8,128)} fusion(f32[1024,1024]{1,0:T(8,128)} %maximum_select_fusion, f32[1024,1024]{0,1:T(8,128)} %copy.9, pred[]{:T(512)S(6)} %eq.19, pred[]{:T(512)S(6)} %gt.3, f32[1,1,1024,1024]{3,2,1,0:T(8,128)} %param.6), kind=kOutput, calls=%fused_computation.3 | convolution fusion | flops 6447693824 | bytes 16777218 | tf_op jit(solution)/shard_map/dot_general | solution.py:345
  136.3 0.7 slice_bitcast_fusion.4
  137.0 31.1 %all-gather = f32[128,1,128]{2,1,0:T(1,128)S(1)} all-gather(f32[1,1,128]{2,1,0:T(1,128)S(1)} %slice_bitcast_fusion.4), channel_id=1, replica_groups=mesh['dp'=4,'block'=32] {'dp','block'}, dimensions={0}, use_global_device_ids=true | all-gather | bytes 66048 | tf_op jit(solution)/shard_map/all_gather | solution.py:331
  168.2 0.2 slice_reduce_fusion
  168.3 0.1 reshape_squeeze.8
  168.4 0.1 sqrt.14
  168.5 0.1 reshape_squeeze.7
  168.7 0.1 sqrt.12
  168.7 0.6 div.22.scale_ref
  169.3 0.0 all-to-all-done.2.back_ref
  169.3 3.1 %collect.1 = f32[8,28672]{1,0:T(8,128)} custom-call(s32[28]{0:T(128)} %owners_ref.5, f32[64]{0:T(128)} %div.22.scale_ref, f32[64,8,1024]{2,1,0:T(8,128)} %all-to-all-done.2.back_ref), custom_call_target="tpu_custom_call" | custom-call | bytes 3145728 | tf_op jit(solution)/shard_map/collect/pallas_call | solution.py:115
  (4 shorter events, 0.1 us)
Async XLA Ops:
  0.6 15.5 %copy-start.3 = (f32[8,28672]{1,0:T(8,128)S(1)}, f32[8,28672]{1,0:T(8,128)}, u32[]{:S(2)}) copy-start(f32[8,28672]{1,0:T(8,128)} %grad_ref.1) | copy-start | bytes 2752516
  3.9 41.0 %all-to-all-start = ((f32[64,8,1024]{2,1,0:T(8,128)}), f32[64,8,1024]{2,1,0:T(8,128)S(1)}, u32[]{:S(2)}, u32[]{:S(2)}) async-start(f32[64,8,1024]{2,1,0:T(8,128)} %deal.2), calls=%async_computation | async-start | bytes 4194304 | tf_op jit(solution)/shard_map/all_to_all | solution.py:312
  16.1 21.6 %collective-permute-start = (f32[8,28672]{1,0:T(8,128)S(1)}, f32[8,28672]{1,0:T(8,128)S(1)}, u32[]{:S(2)}, u32[]{:S(2)}) collective-permute-start(f32[8,28672]{1,0:T(8,128)S(1)} %copy-done.3), channel_id=1, source_target_pairs={{0,32},{32,0},{64,96},{96,64},{1,33},{33,1},{65,97},{97,65},{2,34}... | collective-permute-start | bytes 2752520 | tf_op jit(solution)/shard_map/ppermute | solution.py:317
  33.9 19.1 %copy-start.5 = (s32[28]{0:T(128)S(1)}, s32[28]{0:T(128)}, u32[]{:S(2)}) copy-start(s32[28]{0:T(128)} %owners_ref.5) | copy-start | bytes 340
  33.9 20.5 %copy-start.6 = (s32[4]{0:T(128)S(1)}, s32[4]{0:T(128)}, u32[]{:S(2)}) copy-start(s32[4]{0:T(128)} %constant.52.clone) | copy-start | bytes 52
  33.9 20.5 %copy-start.7 = (s32[4]{0:T(128)S(1)}, s32[4]{0:T(128)}, u32[]{:S(2)}) copy-start(s32[4]{0:T(128)} %constant.53.clone) | copy-start | bytes 52
  37.6 0.9 copy-start.4
  37.6 46.5 %collective-permute-start.1 = (f32[2064,256]{1,0:T(8,128)}, f32[2064,256]{1,0:T(8,128)}, u32[]{:S(2)}, u32[]{:S(2)}) collective-permute-start(f32[2064,256]{1,0:T(8,128)} %get-tuple-element.13), channel_id=1, source_target_pairs={{0,32},{32,0},{64,96},{96,64},{1,33},{33,1},{65,97},{97,65},{2,34}... | collective-permute-start | bytes 6340616 | tf_op jit(solution)/shard_map/ppermute | solution.py:317
  44.9 11.4 %copy-start = (f32[64,8,1024]{2,1,0:T(8,128)}, f32[64,8,1024]{2,1,0:T(8,128)S(1)}, u32[]{:S(2)}) copy-start(f32[64,8,1024]{2,1,0:T(8,128)S(1)} %all-to-all-done) | copy-start | bytes 6291460
  44.9 36.8 %all-to-all-start.1 = ((f32[64,8,1024]{2,1,0:T(8,128)}), f32[64,8,1024]{2,1,0:T(8,128)}, u32[]{:S(2)}, u32[]{:S(2)}) async-start(f32[64,8,1024]{2,1,0:T(8,128)} %deal.3), calls=%async_computation.1 | async-start | bytes 4194304 | tf_op jit(solution)/shard_map/all_to_all | solution.py:312
  97.5 14.3 %copy-start.1 = (f32[64,8,1024]{2,1,0:T(8,128)S(1)}, f32[64,8,1024]{2,1,0:T(8,128)}, u32[]{:S(2)}) copy-start(f32[64,8,1024]{2,1,0:T(8,128)} %copy-done) | copy-start | bytes 6291460
  97.5 71.8 %all-to-all-start.2 = ((f32[64,8,1024]{2,1,0:T(8,128)}), f32[64,8,1024]{2,1,0:T(8,128)}, u32[]{:S(2)}, u32[]{:S(2)}) async-start(f32[64,8,1024]{2,1,0:T(8,128)} %bitcast.27), calls=%async_computation.2 | async-start | bytes 4194304 | tf_op jit(solution)/shard_map/all_to_all | solution.py:312
  110.0 1.9 %copy-start.2 = (f32[256,1024]{1,0:T(8,128)S(1)}, f32[256,1024]{1,0:T(8,128)}, u32[]{:S(2)}) copy-start(f32[256,1024]{1,0:T(8,128)} %get-tuple-element.21) | copy-start | bytes 3145732
where the time goes:
time: 173 us; the launch traced here: 172 us
  Pallas kernels  40.7 us (24%)
  waiting for transfers between devices  34.7 us (20%)
  starting transfers between devices  32.9 us (19%)
  blocking collectives  31.1 us (18%)
  matrix products  15.4 us (9%)
  local copies, waits for them, and re-layouts  10.5 us (6%)
  other arithmetic  5.68 us (3%)
    all_to_all x3, starting transfers between devices, exchange(): lax.all_to_all(x, BOTH, split_axis=0, concat_axis=0, tiled=True, axis_ind...  32.8 us
    all_gather x1, blocking collectives, per_device(): all_sums = lax.all_gather(sums[0], BOTH)  31.1 us
    all_to_all x3, waiting for transfers between devices, exchange(): lax.all_to_all(x, BOTH, split_axis=0, concat_axis=0, tiled=True, axis_ind...  28.5 us
    pallas_call x1, Pallas kernels, root(): pl.pallas_call(root_kernel, out_shape=[half, half, jax.ShapeDtypeStruct((...  17.7 us
    dot_general x1, matrix products, per_device(): lax.dot_general(flipped, flipped, (((1,), (1,)), ((), ())), precision=lax...  15.4 us
    pallas_call x1, Pallas kernels, apply_roots(): pl.pallas_call(apply_kernel, out_shape=[jax.ShapeDtypeStruct((half, size)...  13.4 us
    pallas_call x2, Pallas kernels, deal(): pl.pallas_call(deal_kernel, out_shape=jax.ShapeDtypeStruct((2 * owner_cou...  6.44 us
    ppermute x2, waiting for transfers between devices, swap(): return lax.ppermute(x, 'dp', [(i, i ^ 1) for i in range(4)])  6.15 us
  transfers between devices with their start and end apart: 5, of which 4 were waited for; matrix products, arithmetic and copies ran while one was open for 18% of the time, Pallas kernels for 12%

commit v1 on v0

v1 whole, which is shorter than its diff:
```python
import jax
import jax.numpy as jnp
from jax import lax
from jax.experimental import pallas as pl
from jax.experimental.pallas import tpu as pltpu
from jax.sharding import PartitionSpec as P

BOTH = ("dp", "block")
TILE = 256
VMEM_LIMIT = 56 * 1024 * 1024

decay_rate = 0.9
epsilon = 1e-06


def vmem():
    return pl.BlockSpec(memory_space=pltpu.VMEM)


def anywhere():
    return pl.BlockSpec(memory_space=pl.ANY)


def smem():
    return pl.BlockSpec(memory_space=pltpu.SMEM)


def diag_mask():
    rows = lax.broadcasted_iota(jnp.int32, (TILE, TILE), 0)
    cols = lax.broadcasted_iota(jnp.int32, (TILE, TILE), 1)
    return rows, cols


def span(index):
    return slice(index * TILE, (index + 1) * TILE)


def split(value):
    high = value.astype(jnp.bfloat16)
    low = (value - high.astype(jnp.float32)).astype(jnp.bfloat16)
    return high, low


def dot3(a_high, a_low, b_high, b_low):
    def one(a, b):
        return jnp.dot(a, b, preferred_element_type=jnp.float32)

    return one(a_high, b_high) + (one(a_high, b_low) + one(a_low, b_high))


def put_split(high_ref, low_ref, i, j, block):
    high, low = split(block)
    high_ref[span(i), span(j)] = high
    low_ref[span(i), span(j)] = low


def put_both(high_ref, low_ref, i, j, block):
    put_split(high_ref, low_ref, i, j, block)
    if i != j:
        put_split(high_ref, low_ref, j, i, block.T)


def place_of(owners_ref, count_ref, c):
    owner = owners_ref[c]
    slot = count_ref[owner]
    count_ref[owner] = slot + 1
    return slot * count_ref.shape[0] + owner


def clear(count_ref):
    @pl.loop(0, count_ref.shape[0])
    def _(o):
        count_ref[o] = 0


def column_copies(count, width, source, target, sems):
    each = -(-count // sems.shape[0])
    copies = []
    for k, first in enumerate(range(0, count, each)):
        cols = slice(first * width, min(first + each, count) * width)
        copies.append(pltpu.make_async_copy(source.at[:, cols], target.at[:, cols], sems.at[k]))
    return each, copies


def deal_kernel(owners_ref, grad_hbm, out_hbm, count_ref, buffer, sems, whole_sems):
    width = out_hbm.shape[-1]
    count = owners_ref.shape[0]
    each, loads = column_copies(count, width, grad_hbm, buffer, whole_sems)
    for load in loads:
        load.start()
    clear(count_ref)
    stores = []
    for c in range(count):
        place = place_of(owners_ref, count_ref, c)
        if c % each == 0:
            loads[c // each].wait()
        cols = slice(c * width, (c + 1) * width)
        stores.append(pltpu.make_async_copy(buffer.at[:, cols], out_hbm.at[place], sems.at[c]))
        stores[-1].start()
    for store in stores:
        store.wait()


def collect_kernel(owners_ref, back_hbm, out_hbm, count_ref, buffer, sems, whole_sems):
    width = back_hbm.shape[-1]
    count = owners_ref.shape[0]
    clear(count_ref)
    loads = []
    for c in range(count):
        place = place_of(owners_ref, count_ref, c)
        cols = slice(c * width, (c + 1) * width)
        loads.append(pltpu.make_async_copy(back_hbm.at[place], buffer.at[:, cols], sems.at[c]))
        loads[-1].start()
    each, stores = column_copies(count, width, buffer, out_hbm, whole_sems)
    for k, store in enumerate(stores):
        for load in loads[k * each : (k + 1) * each]:
            load.wait()
        store.start()
    for store in stores:
        store.wait()


def move_blocks(kernel, name, owners, source, owner_count, shape, flat):
    return pl.pallas_call(
        kernel,
        out_shape=jax.ShapeDtypeStruct(shape, jnp.float32),
        in_specs=[smem(), anywhere()],
        out_specs=anywhere(),
        scratch_shapes=[
            pltpu.SMEM((owner_count,), jnp.int32),
            pltpu.VMEM(flat, jnp.float32),
            pltpu.SemaphoreType.DMA((owners.shape[0],)),
            pltpu.SemaphoreType.DMA((4,)),
        ],
        cost_estimate=pl.CostEstimate(flops=0, bytes_accessed=2 * 2**20, transcendentals=0),
        name=name,
    )(owners, source)


def deal(owners, grad, owner_count):
    rows = grad.shape[0]
    width = grad.shape[1] // owners.shape[0]
    return move_blocks(deal_kernel, "deal", owners, grad, owner_count, (2 * owner_count, rows, width), grad.shape)


def collect(owners, back):
    places, rows, width = back.shape
    shape = (rows, owners.shape[0] * width)
    return move_blocks(collect_kernel, "collect", owners, back, places // 2, shape, shape)


def lower_blocks(tiles):
    return [(i, j) for j in range(tiles) for i in range(j + 1, tiles)]


def root_kernel(a_ref, xh_ref, xl_ref, pack_ref, sh, sl, s2, s2h, s2l, s3h, s3l, qh, ql):
    size = a_ref.shape[0]
    tiles = size // TILE
    rows, cols = diag_mask()
    on_diag = rows == cols
    trace = jnp.float32(0.0)
    for b in range(tiles):
        trace += jnp.sum(jnp.where(on_diag, a_ref[span(b), span(b)], 0.0))
    shrink = 0.25 / (2.0 * trace / size)

    def step_block(i, j):
        block = a_ref[span(i), span(j)] * -shrink
        if i == j:
            block = jnp.where(on_diag, 1.25 + block, block)
        return block

    for i in range(tiles):
        for j in range(tiles):
            put_split(sh, sl, i, j, step_block(i, j))

    def product(ah, al, bh, bl, j):
        low_rows = slice(j * TILE, size)
        return dot3(ah[low_rows, :], al[low_rows, :], bh[:, span(j)], bl[:, span(j)])

    for j in range(tiles):
        column = product(sh, sl, sh, sl, j)
        s2[j * TILE :, span(j)] = column
        for i in range(j, tiles):
            put_both(s2h, s2l, i, j, column[span(i - j)])
    for j in range(tiles):
        column = product(sh, sl, s2h, s2l, j)
        for i in range(j, tiles):
            block = column[span(i - j)]
            put_both(s3h, s3l, i, j, block)
            put_both(qh, ql, i, j, block - 1.25 * s2[span(i), span(j)])
    for j in range(tiles):
        column = product(s3h, s3l, qh, ql, j)
        for i in range(j, tiles):
            block = column[span(i - j)] + 1.25 * step_block(i, j)
            put_both(xh_ref, xl_ref, i, j, block)
            if i != j:
                pack_ref[span(lower_blocks(tiles).index((i, j)))] = block
            else:
                s2[span(i), span(i)] = block
    offset = len(lower_blocks(tiles))
    last = (offset + tiles // 2) * TILE
    for pair in range(tiles // 2):
        first = s2[span(2 * pair), span(2 * pair)]
        second = s2[span(2 * pair + 1), span(2 * pair + 1)]
        pack_ref[span(offset + pair)] = jnp.where(rows >= cols, first, second)
        diagonal = jnp.sum(jnp.where(on_diag, second, 0.0), axis=0, keepdims=True)
        pack_ref[last + pair * 8 : last + pair * 8 + 8] = jnp.broadcast_to(diagonal, (8, TILE))


def packed_rows(size):
    tiles = size // TILE
    return (len(lower_blocks(tiles)) + tiles // 2) * TILE + 8 * (tiles // 2)


def root(factor):
    size = factor.shape[0]
    half = jax.ShapeDtypeStruct((size, size), jnp.bfloat16)
    return pl.pallas_call(
        root_kernel,
        out_shape=[half, half, jax.ShapeDtypeStruct((packed_rows(size), TILE), jnp.float32)],
        in_specs=[vmem()],
        out_specs=[vmem()] * 3,
        scratch_shapes=[pltpu.VMEM((size, size), jnp.bfloat16)] * 2
        + [pltpu.VMEM((size, size), jnp.float32)]
        + [pltpu.VMEM((size, size), jnp.bfloat16)] * 6,
        compiler_params=pltpu.CompilerParams(vmem_limit_bytes=VMEM_LIMIT),
        cost_estimate=pl.CostEstimate(
            flops=0, bytes_accessed=0, transcendentals=0
        ),
        name="root",
    )(factor)


def unpack_block(pack_ref, tiles, i, j, rows, cols):
    if i != j:
        return pack_ref[span(lower_blocks(tiles).index((i, j)))]
    offset = len(lower_blocks(tiles))
    last = (offset + tiles // 2) * TILE
    both = pack_ref[span(offset + i // 2)]
    if i % 2 == 0:
        return jnp.where(rows >= cols, both, both.T)
    diagonal = pack_ref[last + (i // 2) * 8 : last + (i // 2) * 8 + 1]
    return jnp.where(rows == cols, diagonal, jnp.where(rows < cols, both, both.T))


def split_kernel(x_ref, high_ref, low_ref, sum_ref):
    half, size = x_ref.shape
    total = jnp.zeros((8, TILE), jnp.float32)
    for r in range(half // TILE):
        for c in range(size // TILE):
            block = x_ref[span(r), span(c)]
            put_split(high_ref, low_ref, r, c, block)
            total += jnp.sum((block * block).reshape(TILE // 8, 8, TILE), axis=0)
    sum_ref[...] = jnp.full(sum_ref.shape, jnp.sum(total), jnp.float32)


def split_rows(x):
    half = jax.ShapeDtypeStruct(x.shape, jnp.bfloat16)
    return pl.pallas_call(
        split_kernel,
        out_shape=[half, half, jax.ShapeDtypeStruct((8, 128), jnp.float32)],
        in_specs=[vmem()],
        out_specs=[vmem()] * 3,
        compiler_params=pltpu.CompilerParams(vmem_limit_bytes=VMEM_LIMIT),
        cost_estimate=pl.CostEstimate(flops=0, bytes_accessed=4 * 2**20, transcendentals=0),
        name="split_rows",
    )(x)


def near_kernel(
    place_ref, xh_ref, xl_ref, pack_ref, nh_ref, nl_ref, v_ref, fh_ref, fl_ref, rh, rl, ph, pw, lh, ll
):
    size = xh_ref.shape[0]
    tiles = size // TILE
    side = place_ref[0]
    rows, cols = diag_mask()

    def place_left(high_ref, low_ref):
        for r in range(2):
            source_rows = pl.ds(pl.multiple_of(place_ref[1 + r] * TILE, TILE), TILE)
            for c in range(tiles):
                source_cols = pl.ds(pl.multiple_of(place_ref[1 + c] * TILE, TILE), TILE)
                to_high, to_low = (lh, ll) if c < 2 else (fh_ref, fl_ref)
                to_high[span(r), span(c % 2)] = high_ref[source_rows, source_cols]
                to_low[span(r), span(c % 2)] = low_ref[source_rows, source_cols]

    def unpack(high_ref, low_ref):
        for i in range(tiles):
            for j in range(i + 1):
                put_both(high_ref, low_ref, i, j, unpack_block(pack_ref, tiles, i, j, rows, cols))

    @pl.when(side == 0)
    def _():
        place_left(xh_ref, xl_ref)
        unpack(rh, rl)

    @pl.when(side != 0)
    def _():
        unpack(ph, pw)
        place_left(ph, pw)
        rh[...] = xh_ref[...]
        rl[...] = xl_ref[...]

    for j in range(tiles):
        v_ref[:, span(j)] = dot3(lh[...], ll[...], nh_ref[:, span(j)], nl_ref[:, span(j)])


def near_part(place, x_high, x_low, pack, near_high, near_low):
    size = x_high.shape[0]
    half = size // 2
    big = pltpu.VMEM((size, size), jnp.bfloat16)
    small = pltpu.VMEM((half, half), jnp.bfloat16)
    full_out = jax.ShapeDtypeStruct((size, size), jnp.bfloat16)
    quarter_out = jax.ShapeDtypeStruct((half, half), jnp.bfloat16)
    return pl.pallas_call(
        near_kernel,
        out_shape=[
            jax.ShapeDtypeStruct((half, size), jnp.float32),
            quarter_out, quarter_out, full_out, full_out,
        ],
        in_specs=[smem()] + [vmem()] * 5,
        out_specs=[vmem()] * 5,
        scratch_shapes=[big, big, small, small],
        compiler_params=pltpu.CompilerParams(vmem_limit_bytes=VMEM_LIMIT),
        cost_estimate=pl.CostEstimate(
            flops=3 * size**3, bytes_accessed=12 * 2**20, transcendentals=0
        ),
        name="near_part",
    )(place, x_high, x_low, pack, near_high, near_low)


def far_kernel(
    far_hbm, lh_hbm, ll_hbm, v_hbm, rh_hbm, rl_hbm, near_sum_ref, raw_hbm, gh_hbm, gl_hbm, sums_ref,
    far, lh, ll, v, rh, rl, gh, gl, uh, ul, raw, in_sems, out_sems,
):
    half, size = far.shape
    tiles = size // TILE
    sources = (far_hbm, lh_hbm, ll_hbm, v_hbm, rh_hbm, rl_hbm)
    loads = [
        pltpu.make_async_copy(source, target, in_sems.at[k])
        for k, (source, target) in enumerate(zip(sources, (far, lh, ll, v, rh, rl)))
    ]
    for load in loads:
        load.start()
    for load in loads[:4]:
        load.wait()
    total = jnp.zeros((8, TILE), jnp.float32)
    for j in range(tiles):
        block = far[:, span(j)]
        high, low = split(block)
        gh[:, span(j)] = high
        gl[:, span(j)] = low
        total += jnp.sum((block * block).reshape(half // 8, 8, TILE), axis=0)
        column = v[:, span(j)] + dot3(lh[...], ll[...], high, low)
        high, low = split(column)
        uh[:, span(j)] = high
        ul[:, span(j)] = low
    stores = [
        pltpu.make_async_copy(gh, gh_hbm, out_sems.at[tiles]),
        pltpu.make_async_copy(gl, gl_hbm, out_sems.at[tiles + 1]),
    ]
    for store in stores:
        store.start()
    grad_sum = jnp.sum(total) + near_sum_ref[0, 0]
    for load in loads[4:]:
        load.wait()
    total = jnp.zeros((8, TILE), jnp.float32)
    for j in range(tiles):
        column = dot3(uh[...], ul[...], rh[:, span(j)], rl[:, span(j)])
        raw[:, span(j)] = column
        stores.append(
            pltpu.make_async_copy(raw.at[:, span(j)], raw_hbm.at[:, span(j)], out_sems.at[j])
        )
        stores[-1].start()
        total += jnp.sum((column * column).reshape(half // 8, 8, TILE), axis=0)
    raw_sum = jnp.sum(total)
    lane = lax.broadcasted_iota(jnp.int32, (8, 128), 1)
    sums_ref[...] = jnp.where(lane == 0, raw_sum, grad_sum)
    for store in stores:
        store.wait()


def far_part(far, left_high, left_low, v, right_high, right_low, near_sum):
    half, size = far.shape
    tiles = size // TILE
    wide = pltpu.VMEM((half, size), jnp.bfloat16)
    wide_f32 = pltpu.VMEM((half, size), jnp.float32)
    square = pltpu.VMEM((half, half), jnp.bfloat16)
    big = pltpu.VMEM((size, size), jnp.bfloat16)
    wide_out = jax.ShapeDtypeStruct((half, size), jnp.bfloat16)
    return pl.pallas_call(
        far_kernel,
        out_shape=[
            jax.ShapeDtypeStruct((half, size), jnp.float32),
            wide_out,
            wide_out,
            jax.ShapeDtypeStruct((8, 128), jnp.float32),
        ],
        in_specs=[anywhere()] * 6 + [vmem()],
        out_specs=[anywhere()] * 3 + [vmem()],
        scratch_shapes=[
            wide_f32, square, square, wide_f32, big, big, wide, wide, wide, wide, wide_f32,
            pltpu.SemaphoreType.DMA((6,)),
            pltpu.SemaphoreType.DMA((tiles + 2,)),
        ],
        compiler_params=pltpu.CompilerParams(vmem_limit_bytes=VMEM_LIMIT),
        cost_estimate=pl.CostEstimate(
            flops=5 * size**3, bytes_accessed=12 * 2**20, transcendentals=0
        ),
        name="far_part",
    )(far, left_high, left_low, v, right_high, right_low, near_sum)


def graft_kernel(own_ref, other_ref, raw_hbm, out_hbm, buffer, in_sems, out_sems):
    half, size = buffer.shape
    steps = in_sems.shape[0]
    count = size * size
    loads, stores = [], []
    for k in range(steps):
        rows = slice(k * half // steps, (k + 1) * half // steps)
        loads.append(pltpu.make_async_copy(raw_hbm.at[rows], buffer.at[rows], in_sems.at[k]))
        stores.append(pltpu.make_async_copy(buffer.at[rows], out_hbm.at[rows], out_sems.at[k]))
    for load in loads:
        load.start()
    own = own_ref[...]
    raw_sum = own[:1, :1] + other_ref[:1, :1]
    grad_sum = own[:1, 1:2]
    scale = jnp.sqrt(grad_sum / count + epsilon) / jnp.sqrt(raw_sum / count + epsilon)
    for k in range(steps):
        loads[k].wait()
        rows = slice(k * half // steps, (k + 1) * half // steps)
        buffer[rows] = buffer[rows] * scale
        stores[k].start()
    for store in stores:
        store.wait()


def graft(own_sums, other_sums, raw):
    steps = 4
    return pl.pallas_call(
        graft_kernel,
        out_shape=jax.ShapeDtypeStruct(raw.shape, jnp.float32),
        in_specs=[vmem(), vmem(), anywhere()],
        out_specs=anywhere(),
        scratch_shapes=[
            pltpu.VMEM(raw.shape, jnp.float32),
            pltpu.SemaphoreType.DMA((steps,)),
            pltpu.SemaphoreType.DMA((steps,)),
        ],
        cost_estimate=pl.CostEstimate(flops=0, bytes_accessed=4 * 2**20, transcendentals=0),
        name="graft",
    )(own_sums, other_sums, raw)


def renew_kernel(
    place_ref, a_ref, nh_ref, nl_ref, fh_ref, fl_ref, out_ref, gh, gl, th, tl
):
    size = a_ref.shape[0]
    half = size // 2
    tiles = size // TILE
    side = place_ref[0]
    used = place_ref[1 + tiles] != 0

    for part, (high_ref, low_ref) in enumerate(((nh_ref, nl_ref), (fh_ref, fl_ref))):
        for r in range(half // TILE):
            for c in range(tiles):
                p = part * (half // TILE) + r
                for source, target, flipped in ((high_ref, gh, th), (low_ref, gl, tl)):
                    block = source[span(r), span(c)]
                    target[span(p), span(c)] = block
                    flipped[span(c), span(p)] = block.T

    def write(i, j, block):
        rows = pl.ds(pl.multiple_of(i * TILE, TILE), TILE)
        cols = pl.ds(pl.multiple_of(j * TILE, TILE), TILE)
        gain = jnp.where(used, block * ((1.0 - decay_rate) / size), 0.0)
        out_ref[rows, cols] = decay_rate * a_ref[rows, cols] + gain

    def products(lh, ll, rh, rl, where):
        for j in range(tiles):
            low_rows = slice(j * TILE, size)
            column = dot3(lh[low_rows, :], ll[low_rows, :], rh[:, span(j)], rl[:, span(j)])
            for i in range(j, tiles):
                block = column[span(i - j)]
                write(where(i), where(j), block)
                if i != j:
                    write(where(j), where(i), block.T)

    @pl.when(side == 0)
    def _():
        products(gh, gl, th, tl, lambda i: place_ref[1 + i])

    @pl.when(side != 0)
    def _():
        products(th, tl, gh, gl, lambda i: i)


def renew(place, factor, near_high, near_low, far_high, far_low):
    size = factor.shape[0]
    return pl.pallas_call(
        renew_kernel,
        out_shape=jax.ShapeDtypeStruct((size, size), jnp.float32),
        in_specs=[smem()] + [vmem()] * 5,
        out_specs=vmem(),
        scratch_shapes=[pltpu.VMEM((size, size), jnp.bfloat16)] * 4,
        compiler_params=pltpu.CompilerParams(vmem_limit_bytes=VMEM_LIMIT),
        cost_estimate=pl.CostEstimate(
            flops=4 * size**3, bytes_accessed=12 * 2**20, transcendentals=0
        ),
        name="renew",
    )(place, factor, near_high, near_low, far_high, far_low)


def per_device(grad, factors, owners):
    row_count = grad.shape[0]
    block_size = factors.shape[-1]
    owner_count = lax.axis_size("block")
    dp_index = lax.axis_index("dp")
    blk_index = lax.axis_index("block")
    side = dp_index % 2
    slot = dp_index // 2
    outer_pair = (dp_index == 0) | (dp_index == 3)
    groups = [
        [x * owner_count + b for x in pair for b in range(owner_count)] for pair in ((0, 3), (1, 2))
    ]

    def exchange(x):
        return lax.all_to_all(
            x, BOTH, split_axis=0, concat_axis=0, tiled=True, axis_index_groups=groups
        )

    def swap(x):
        return lax.ppermute(x, "dp", [(i, i ^ 1) for i in range(4)])

    order = jnp.where(outer_pair, jnp.array([0, 3, 1, 2]), jnp.array([1, 2, 0, 3]))
    used = jnp.sum(owners == blk_index) > slot
    place = jnp.concatenate([side[None], order, used[None]]).astype(jnp.int32)

    other_grad = swap(grad)
    near = exchange(deal(owners, grad, owner_count)).reshape(block_size // 2, block_size)
    own_factor = factors[0, 0]
    x_high, x_low, pack = root(own_factor)
    other_pack = swap(pack)
    dealt = deal(owners, other_grad, owner_count)
    near, dealt = lax.optimization_barrier((near, dealt))
    far = exchange(dealt).reshape(block_size // 2, block_size)

    near_high, near_low, near_sum = split_rows(near)
    v, left_high, left_low, right_high, right_low = near_part(
        place, x_high, x_low, other_pack, near_high, near_low
    )
    raw, far_high, far_low, sums = far_part(
        far, left_high, left_low, v, right_high, right_low, near_sum
    )
    scaled = graft(sums, swap(sums), raw)
    scaled, far_high, far_low = lax.optimization_barrier((scaled, far_high, far_low))
    back = exchange(scaled.reshape(2 * owner_count, row_count, block_size))
    update = collect(owners, back)
    new_own = renew(place, own_factor, near_high, near_low, far_high, far_low)
    return (new_own[None, None], update)


def solution(mesh):
    placed = (P(BOTH, None), P("dp", "block", None, None), P())
    return jax.shard_map(
        per_device,
        mesh=mesh,
        in_specs=placed,
        out_specs=(P("dp", "block", None, None), P(BOTH, None)),
        check_vma=False,
    )
```

time: 173 us -> 154 us (0.89)
  blocking collectives: 31.1 us -> 0 us
  Pallas kernels: 40.7 us -> 62.9 us
  matrix products: 15.4 us -> 0 us
  waiting for transfers between devices: 34.7 us -> 49.4 us
  local copies, waits for them, and re-layouts: 10.5 us -> 3.27 us
  other arithmetic: 5.68 us -> 1.28 us
    all_gather x1 -> x0, blocking collectives: 31.1 us -> none  [per_device(): all_sums = lax.all_gather(sums[0], BOTH)]
    pallas_call x4 -> x8, Pallas kernels: 22.9 us -> 45.2 us  [the longest x1 11.8 us: renew(): pl.pallas_call(renew_kernel, out_shape=jax.ShapeDtypeStruct((size, size),...]
    ppermute x2 -> x3, waiting for transfers between devices: 6.15 us -> 28.2 us  [swap(): return lax.ppermute(x, 'dp', [(i, i ^ 1) for i in range(4)])]
    dot_general x1 -> x0, matrix products: 15.4 us -> none  [per_device(): lax.dot_general(flipped, flipped, (((1,), (1,)), ((), ())), precision=lax...]
    all_to_all x3, waiting for transfers between devices: 28.5 us -> 21.2 us  [exchange(): lax.all_to_all(x, BOTH, split_axis=0, concat_axis=0, tiled=True, axis_ind...]
    select_n x1 -> x0, local copies, waits for them, and re-layouts: 5.38 us -> none  [per_device(): jnp.where(outer_pair, jnp.concatenate([near[:quarter], far, near[quarter:...]
    select_n x1 -> x0, other arithmetic: 3.71 us -> none  [per_device(): jnp.where(outer_pair, jnp.concatenate([near[:quarter], far, near[quarter:...]
    slice x3 -> x0, local copies, waits for them, and re-layouts: 3.22 us -> none  [the longest x1 1.86 us: per_device(): far[:quarter]]
  transfers between devices with their start and end apart: 5 -> 6, of which waited for: 4 -> 5; matrix products, arithmetic and copies ran while one was open for 18% -> 1% of each run, Pallas kernels for 12% -> 28%
where the time goes in v1:
time: 154 us; the launch traced here: 153 us
  Pallas kernels  62.9 us (41%)
  waiting for transfers between devices  49.4 us (32%)
  starting transfers between devices  34.6 us (22%)
  local copies, waits for them, and re-layouts  3.27 us (2%)
  between operations  1.62 us (1%)
    all_to_all x3, starting transfers between devices, exchange(): lax.all_to_all(x, BOTH, split_axis=0, concat_axis=0, tiled=True, axis_ind...  32.7 us
    ppermute x3, waiting for transfers between devices, swap(): return lax.ppermute(x, 'dp', [(i, i ^ 1) for i in range(4)])  28.2 us
    all_to_all x3, waiting for transfers between devices, exchange(): lax.all_to_all(x, BOTH, split_axis=0, concat_axis=0, tiled=True, axis_ind...  21.2 us
    pallas_call x1, Pallas kernels, root(): pl.pallas_call(root_kernel, out_shape=[half, half, jax.ShapeDtypeStruct((...  17.7 us
    pallas_call x1, Pallas kernels, renew(): pl.pallas_call(renew_kernel, out_shape=jax.ShapeDtypeStruct((size, size),...  11.8 us
    pallas_call x1, Pallas kernels, far_part(): pl.pallas_call(far_kernel, out_shape=[jax.ShapeDtypeStruct((half, size),...  10.2 us
    pallas_call x3, Pallas kernels, move_blocks(): pl.pallas_call(kernel, out_shape=jax.ShapeDtypeStruct(shape, jnp.float32)...  8.86 us
    pallas_call x1, Pallas kernels, near_part(): pl.pallas_call(near_kernel, out_shape=[jax.ShapeDtypeStruct((half, size),...  7.5 us
  transfers between devices with their start and end apart: 6, of which 5 were waited for; matrix products, arithmetic and copies ran while one was open for 1% of the time, Pallas kernels for 28%

profile of v1, /device:TPU:1, one launch (start us, length us, event | category | flops | bytes accessed | tf_op | source)
XLA Modules:
  0.0 153.1 jit_solution(4135282499887057899)
XLA Ops:
  0.6 3.0 %deal.2 = f32[64,8,1024]{2,1,0:T(8,128)} custom-call(s32[28]{0:T(128)} %owners_ref.5, f32[8,28672]{1,0:T(8,128)} %grad_hbm.1), custom_call_target="tpu_custom_call" | custom-call | bytes 2097152 | tf_op jit(solution)/shard_map/deal/pallas_call | solution.py:124
  3.6 0.0 copy-start.2
  3.6 12.3 %all-to-all-start = ((f32[64,8,1024]{2,1,0:T(8,128)}), f32[64,8,1024]{2,1,0:T(8,128)S(1)}, u32[]{:S(2)}, u32[]{:S(2)}) async-start(f32[64,8,1024]{2,1,0:T(8,128)} %deal.2), calls=%async_computation | async-start | bytes 4194304 | tf_op jit(solution)/shard_map/all_to_all | solution.py:528
  16.0 0.0 copy-done.2
  16.0 0.1 collective-permute-start
  16.1 17.7 %root.1 = (bf16[1024,1024]{1,0:T(8,128)(2,1)}, bf16[1024,1024]{1,0:T(8,128)(2,1)}, f32[2064,256]{1,0:T(8,128)}) custom-call(f32[1024,1024]{1,0:T(8,128)} %bitcast.9), custom_call_target="tpu_custom_call" | custom-call | tf_op jit(solution)/shard_map/root/pallas_call | solution.py:218
  33.8 1.4 collective-permute-start.1
  35.3 2.4 %collective-permute-done.grad_hbm = f32[8,28672]{1,0:T(8,128)} collective-permute-done((f32[8,28672]{1,0:T(8,128)S(1)}, f32[8,28672]{1,0:T(8,128)}, u32[]{:S(2)}, u32[]{:S(2)}) %collective-permute-start) | collective-permute-done | bytes 917536 | tf_op jit(solution)/shard_map/ppermute | solution.py:533
  37.6 2.9 %deal.3 = f32[64,8,1024]{2,1,0:T(8,128)} custom-call(s32[28]{0:T(128)} %owners_ref.5, f32[8,28672]{1,0:T(8,128)} %collective-permute-done.grad_hbm), custom_call_target="tpu_custom_call" | custom-call | bytes 2097152 | tf_op jit(solution)/shard_map/deal/pallas_call | solution.py:124
  40.5 4.2 %all-to-all-done = f32[64,8,1024]{2,1,0:T(8,128)S(1)} async-done(((f32[64,8,1024]{2,1,0:T(8,128)}), f32[64,8,1024]{2,1,0:T(8,128)S(1)}, u32[]{:S(2)}, u32[]{:S(2)}) %all-to-all-start) | async-done | bytes 2097184 | tf_op jit(solution)/shard_map/all_to_all | solution.py:528
  44.7 0.0 copy-start
  44.7 0.0 copy-start.3
  44.7 0.0 copy-start.5
  44.7 0.0 copy-start.6
  44.7 1.3 copy-done
  46.1 7.9 %all-to-all-start.1 = ((f32[64,8,1024]{2,1,0:T(8,128)}), f32[64,8,1024]{2,1,0:T(8,128)}, u32[]{:S(2)}, u32[]{:S(2)}) async-start(f32[64,8,1024]{2,1,0:T(8,128)} %deal.3), calls=%async_computation.1 | async-start | bytes 4194304 | tf_op jit(solution)/shard_map/all_to_all | solution.py:528
  53.9 0.0 copy-done.3
  54.0 0.6 fusion
  55.3 0.0 copy-done.5
  55.3 0.0 copy-done.6
  55.3 0.6 pad_add_fusion.place_ref
  55.9 3.6 %split_rows.1 = (bf16[512,1024]{1,0:T(8,128)(2,1)}, bf16[512,1024]{1,0:T(8,128)(2,1)}, f32[8,128]{1,0:T(8,128)}) custom-call(f32[512,1024]{1,0:T(8,128)} %bitcast.7), custom_call_target="tpu_custom_call" | custom-call | bytes 4194304 | tf_op jit(solution)/shard_map/split_rows/pallas_call | solution.py:259
  59.5 23.4 %collective-permute-done.1.pack_ref = f32[2064,256]{1,0:T(8,128)} collective-permute-done((f32[2064,256]{1,0:T(8,128)}, f32[2064,256]{1,0:T(8,128)}, u32[]{:S(2)}, u32[]{:S(2)}) %collective-permute-start.1) | collective-permute-done | bytes 2113568 | tf_op jit(solution)/shard_map/ppermute | solution.py:533
  82.9 7.5 %near_part.1 = (f32[512,1024]{1,0:T(8,128)}, bf16[512,512]{1,0:T(8,128)(2,1)}, bf16[512,512]{1,0:T(8,128)(2,1)}, bf16[1024,1024]{1,0:T(8,128)(2,1)}, bf16[1024,1024]{1,0:T(8,128)(2,1)}) custom-call(s32[6]{0:T(128)} %pad_add_fusion.place_ref, bf16[1024,1024]{1,0:T(8,128)(2,1)} %get-tuple-element.26.xh_ref, bf16[1024,1024]{1,0:T(8,128)(2,1)} %get-tuple-element.27.xl_ref, ...), custom_call_target="tpu_custom_call" | custom-call | flops 3221225472 | bytes 12582912 | tf_op jit(solution)/shard_map/near_part/pallas_call | solution.py:315
  90.4 0.0 all-to-all-done.1
  90.4 10.2 %far_part.1 = (f32[512,1024]{1,0:T(8,128)}, bf16[512,1024]{1,0:T(8,128)(2,1)}, bf16[512,1024]{1,0:T(8,128)(2,1)}, f32[8,128]{1,0:T(8,128)}) custom-call(f32[512,1024]{1,0:T(8,128)} %bitcast.4.far_hbm, bf16[512,512]{1,0:T(8,128)(2,1)} %get-tuple-element.29.lh_hbm, bf16[512,512]{1,0:T(8,128)(2,1)} %get-tuple-element.30.ll_hbm, ...), custom_call_target="tpu_custom_call" | custom-call | flops 5368709120 | bytes 12582912 | tf_op jit(solution)/shard_map/far_part/pallas_call | solution.py:391
  100.6 0.3 collective-permute-start.2
  101.0 2.4 %collective-permute-done.2.other_ref = f32[8,128]{1,0:T(8,128)S(1)} collective-permute-done((f32[8,128]{1,0:T(8,128)}, f32[8,128]{1,0:T(8,128)S(1)}, u32[]{:S(2)}, u32[]{:S(2)}) %collective-permute-start.2) | collective-permute-done | bytes 4128 | tf_op jit(solution)/shard_map/ppermute | solution.py:533
  103.4 0.0 copy-start.4
  103.4 0.6 copy-done.4
  104.0 3.3 %graft.1 = f32[512,1024]{1,0:T(8,128)} custom-call(f32[8,128]{1,0:T(8,128)} %get-tuple-element.35.own_ref, f32[8,128]{1,0:T(8,128)} %copy-done.4, f32[512,1024]{1,0:T(8,128)} %get-tuple-element.36.raw_hbm), custom_call_target="tpu_custom_call" | custom-call | bytes 4194304 | tf_op jit(solution)/shard_map/graft/pallas_call | solution.py:440
  107.3 12.5 %all-to-all-start.2 = ((f32[64,8,1024]{2,1,0:T(8,128)}), f32[64,8,1024]{2,1,0:T(8,128)S(1)}, u32[]{:S(2)}, u32[]{:S(2)}) async-start(f32[64,8,1024]{2,1,0:T(8,128)} %bitcast.8), calls=%async_computation.2 | async-start | bytes 4194304 | tf_op jit(solution)/shard_map/all_to_all | solution.py:528
  119.8 11.8 %renew.1 = f32[1024,1024]{1,0:T(8,128)} custom-call(s32[6]{0:T(128)} %pad_add_fusion.place_ref, f32[1024,1024]{1,0:T(8,128)} %bitcast.10, bf16[512,1024]{1,0:T(8,128)(2,1)} %get-tuple-element.23.nh_ref, bf16[512,1024]{1,0:T(8,128)(2,1)} %get-tuple-element.24.nl_ref, bf16[512,1024]{1,0:T(8,128)(2,1)} %get-tuple-element.39.fh_ref, ...), custom_call_target="tpu_custom_call" | custom-call | flops 4294967296 | bytes 12582912 | tf_op jit(solution)/shard_map/renew/pallas_call | solution.py:500
  131.6 17.0 %all-to-all-done.2.back_hbm = f32[64,8,1024]{2,1,0:T(8,128)S(1)} async-done(((f32[64,8,1024]{2,1,0:T(8,128)}), f32[64,8,1024]{2,1,0:T(8,128)S(1)}, u32[]{:S(2)}, u32[]{:S(2)}) %all-to-all-start.2) | async-done | bytes 2097184 | tf_op jit(solution)/shard_map/all_to_all | solution.py:528
  148.6 0.0 copy-start.1
  148.6 1.3 copy-done.1
  149.9 3.0 %collect.1 = f32[8,28672]{1,0:T(8,128)} custom-call(s32[28]{0:T(128)} %owners_ref.5, f32[64,8,1024]{2,1,0:T(8,128)} %copy-done.1), custom_call_target="tpu_custom_call" | custom-call | bytes 2097152 | tf_op jit(solution)/shard_map/collect/pallas_call | solution.py:124
  (1 shorter events, 0.0 us)
Async XLA Ops:
  3.6 12.4 %copy-start.2 = (f32[8,28672]{1,0:T(8,128)S(1)}, f32[8,28672]{1,0:T(8,128)}, u32[]{:S(2)}) copy-start(f32[8,28672]{1,0:T(8,128)} %grad_hbm.1) | copy-start | bytes 2752516
  3.6 41.1 %all-to-all-start = ((f32[64,8,1024]{2,1,0:T(8,128)}), f32[64,8,1024]{2,1,0:T(8,128)S(1)}, u32[]{:S(2)}, u32[]{:S(2)}) async-start(f32[64,8,1024]{2,1,0:T(8,128)} %deal.2), calls=%async_computation | async-start | bytes 4194304 | tf_op jit(solution)/shard_map/all_to_all | solution.py:528
  16.0 21.7 %collective-permute-start = (f32[8,28672]{1,0:T(8,128)S(1)}, f32[8,28672]{1,0:T(8,128)}, u32[]{:S(2)}, u32[]{:S(2)}) collective-permute-start(f32[8,28672]{1,0:T(8,128)S(1)} %copy-done.2), channel_id=1, source_target_pairs={{0,32},{32,0},{64,96},{96,64},{1,33},{33,1},{65,97},{97,65},{2,34}... | collective-permute-start | bytes 2752520 | tf_op jit(solution)/shard_map/ppermute | solution.py:533
  33.8 49.1 %collective-permute-start.1 = (f32[2064,256]{1,0:T(8,128)}, f32[2064,256]{1,0:T(8,128)}, u32[]{:S(2)}, u32[]{:S(2)}) collective-permute-start(f32[2064,256]{1,0:T(8,128)} %get-tuple-element.28), channel_id=1, source_target_pairs={{0,32},{32,0},{64,96},{96,64},{1,33},{33,1},{65,97},{97,65},{2,34}... | collective-permute-start | bytes 6340616 | tf_op jit(solution)/shard_map/ppermute | solution.py:533
  44.7 1.3 copy-start
  44.7 9.2 %copy-start.3 = (s32[28]{0:T(128)S(1)}, s32[28]{0:T(128)}, u32[]{:S(2)}) copy-start(s32[28]{0:T(128)} %owners_ref.5) | copy-start | bytes 340
  44.7 10.5 %copy-start.5 = (s32[4]{0:T(128)S(1)}, s32[4]{0:T(128)}, u32[]{:S(2)}) copy-start(s32[4]{0:T(128)} %constant.41.clone) | copy-start | bytes 52
  44.7 10.5 %copy-start.6 = (s32[4]{0:T(128)S(1)}, s32[4]{0:T(128)}, u32[]{:S(2)}) copy-start(s32[4]{0:T(128)} %constant.40.clone) | copy-start | bytes 52
  46.1 44.4 %all-to-all-start.1 = ((f32[64,8,1024]{2,1,0:T(8,128)}), f32[64,8,1024]{2,1,0:T(8,128)}, u32[]{:S(2)}, u32[]{:S(2)}) async-start(f32[64,8,1024]{2,1,0:T(8,128)} %deal.3), calls=%async_computation.1 | async-start | bytes 4194304 | tf_op jit(solution)/shard_map/all_to_all | solution.py:528
  100.6 2.7 %collective-permute-start.2 = (f32[8,128]{1,0:T(8,128)}, f32[8,128]{1,0:T(8,128)S(1)}, u32[]{:S(2)}, u32[]{:S(2)}) collective-permute-start(f32[8,128]{1,0:T(8,128)} %get-tuple-element.35.own_ref), channel_id=1, source_target_pairs={{0,32},{32,0},{64,96},{96,64},{1,33},{33,1},{65,97},{97,65},{2,34}... | collective-permute-start | bytes 12296 | tf_op jit(solution)/shard_map/ppermute | solution.py:533
  103.4 0.6 copy-start.4
  107.3 41.3 %all-to-all-start.2 = ((f32[64,8,1024]{2,1,0:T(8,128)}), f32[64,8,1024]{2,1,0:T(8,128)S(1)}, u32[]{:S(2)}, u32[]{:S(2)}) async-start(f32[64,8,1024]{2,1,0:T(8,128)} %bitcast.8), calls=%async_computation.2 | async-start | bytes 4194304 | tf_op jit(solution)/shard_map/all_to_all | solution.py:528
  148.6 1.3 copy-start.1

commit v2 on v1

v2 whole, which is shorter than its diff:
```python
import jax
import jax.numpy as jnp
from jax import lax
from jax.experimental import pallas as pl
from jax.experimental.pallas import tpu as pltpu
from jax.sharding import PartitionSpec as P

BOTH = ("dp", "block")
TILE = 256
MIB = 1024 * 1024

decay_rate = 0.9
epsilon = 1e-06


def vmem():
    return pl.BlockSpec(memory_space=pltpu.VMEM)


def anywhere():
    return pl.BlockSpec(memory_space=pl.ANY)


def resident(x):
    return pltpu.with_memory_space_constraint(x, pltpu.VMEM)


def in_hbm(x):
    return pltpu.with_memory_space_constraint(x, pltpu.HBM)


def smem():
    return pl.BlockSpec(memory_space=pltpu.SMEM)


def diag_mask():
    rows = lax.broadcasted_iota(jnp.int32, (TILE, TILE), 0)
    cols = lax.broadcasted_iota(jnp.int32, (TILE, TILE), 1)
    return rows, cols


def span(index):
    return slice(index * TILE, (index + 1) * TILE)


def split(value):
    high = value.astype(jnp.bfloat16)
    low = (value - high.astype(jnp.float32)).astype(jnp.bfloat16)
    return high, low


def dot3(a_high, a_low, b_high, b_low):
    def one(a, b):
        return jnp.dot(a, b, preferred_element_type=jnp.float32)

    return one(a_high, b_high) + (one(a_high, b_low) + one(a_low, b_high))


def put_split(high_ref, low_ref, i, j, block):
    high, low = split(block)
    high_ref[span(i), span(j)] = high
    low_ref[span(i), span(j)] = low


def put_both(high_ref, low_ref, i, j, block):
    put_split(high_ref, low_ref, i, j, block)
    if i != j:
        put_split(high_ref, low_ref, j, i, block.T)


def place_of(owners_ref, count_ref, c):
    owner = owners_ref[c]
    slot = count_ref[owner]
    count_ref[owner] = slot + 1
    return slot * count_ref.shape[0] + owner


def clear(count_ref):
    @pl.loop(0, count_ref.shape[0])
    def _(o):
        count_ref[o] = 0


def column_copies(count, width, source, target, sems):
    each = -(-count // sems.shape[0])
    copies = []
    for k, first in enumerate(range(0, count, each)):
        cols = slice(first * width, min(first + each, count) * width)
        copies.append(pltpu.make_async_copy(source.at[:, cols], target.at[:, cols], sems.at[k]))
    return each, copies


def deal_kernel(owners_ref, grad, out_hbm, count_ref, buffer, sems, whole_sems):
    width = out_hbm.shape[-1]
    count = owners_ref.shape[0]
    each, loads = column_copies(count, width, grad, buffer, whole_sems)
    for load in loads:
        load.start()
    clear(count_ref)
    stores = []
    for c in range(count):
        place = place_of(owners_ref, count_ref, c)
        if c % each == 0:
            loads[c // each].wait()
        cols = slice(c * width, (c + 1) * width)
        stores.append(pltpu.make_async_copy(buffer.at[:, cols], out_hbm.at[place], sems.at[c]))
        stores[-1].start()
    for store in stores:
        store.wait()


def deal_resident_kernel(owners_ref, grad, out_hbm, count_ref, sems):
    width = out_hbm.shape[-1]
    clear(count_ref)
    stores = []
    for c in range(owners_ref.shape[0]):
        place = place_of(owners_ref, count_ref, c)
        cols = slice(c * width, (c + 1) * width)
        stores.append(pltpu.make_async_copy(grad.at[:, cols], out_hbm.at[place], sems.at[c]))
        stores[-1].start()
    for store in stores:
        store.wait()


def collect_kernel(owners_ref, back, out_hbm, count_ref, sems):
    width = back.shape[-1]
    clear(count_ref)
    stores = []
    for c in range(owners_ref.shape[0]):
        place = place_of(owners_ref, count_ref, c)
        cols = slice(c * width, (c + 1) * width)
        stores.append(pltpu.make_async_copy(back.at[place], out_hbm.at[:, cols], sems.at[c]))
        stores[-1].start()
    for store in stores:
        store.wait()


def deal(owners, grad, owner_count, landed):
    rows = grad.shape[0]
    count = owners.shape[0]
    width = grad.shape[1] // count
    counts, sems = pltpu.SMEM((owner_count,), jnp.int32), pltpu.SemaphoreType.DMA((count,))
    buffers = [pltpu.VMEM(grad.shape, jnp.float32), sems, pltpu.SemaphoreType.DMA((4,))]
    return pl.pallas_call(
        deal_resident_kernel if landed else deal_kernel,
        out_shape=pltpu.HBM((2 * owner_count, rows, width), jnp.float32),
        in_specs=[smem(), vmem() if landed else anywhere()],
        out_specs=anywhere(),
        scratch_shapes=[counts, sems] if landed else [counts] + buffers,
        compiler_params=pltpu.CompilerParams(vmem_limit_bytes=16 * MIB),
        cost_estimate=pl.CostEstimate(flops=5 * 10**10, bytes_accessed=2**22, transcendentals=0),
        name="deal",
    )(owners, resident(grad) if landed else in_hbm(grad))


def collect(owners, back):
    places, rows, width = back.shape
    return pl.pallas_call(
        collect_kernel,
        out_shape=jax.ShapeDtypeStruct((rows, owners.shape[0] * width), jnp.float32),
        in_specs=[smem(), vmem()],
        out_specs=anywhere(),
        scratch_shapes=[
            pltpu.SMEM((places // 2,), jnp.int32),
            pltpu.SemaphoreType.DMA((owners.shape[0],)),
        ],
        compiler_params=pltpu.CompilerParams(vmem_limit_bytes=16 * MIB),
        cost_estimate=pl.CostEstimate(flops=0, bytes_accessed=2**22, transcendentals=0),
        name="collect",
    )(owners, resident(back))


def lower_blocks(tiles):
    return [(i, j) for j in range(tiles) for i in range(j + 1, tiles)]


def root_kernel(
    a_hbm, xh_hbm, xl_hbm, pack_hbm,
    a, sh, sl, s2, s2h, s2l, s3h, s3l, qh, ql, xh, xl, pack, in_sems, out_sems,
):
    size = a.shape[0]
    tiles = size // TILE
    rows, cols = diag_mask()
    on_diag = rows == cols
    loads = [
        pltpu.make_async_copy(a_hbm.at[span(b)], a.at[span(b)], in_sems.at[b]) for b in range(tiles)
    ]
    for load in loads:
        load.start()
    diagonal = jnp.zeros((8, TILE), jnp.float32)
    for b in range(tiles):
        loads[b].wait()
        block = jnp.where(on_diag, a[span(b), span(b)], 0.0)
        diagonal += jnp.sum(block.reshape(TILE // 8, 8, TILE), axis=0)
    shrink = 0.25 / (2.0 * jnp.sum(diagonal) / size)

    def step_block(i, j):
        block = a[span(i), span(j)] * -shrink
        if i == j:
            block = jnp.where(on_diag, 1.25 + block, block)
        return block

    for i in range(tiles):
        for j in range(tiles):
            put_split(sh, sl, i, j, step_block(i, j))

    def product(ah, al, bh, bl, j):
        low_rows = slice(j * TILE, size)
        return dot3(ah[low_rows, :], al[low_rows, :], bh[:, span(j)], bl[:, span(j)])

    for j in range(tiles):
        column = product(sh, sl, sh, sl, j)
        s2[j * TILE :, span(j)] = column
        for i in range(j, tiles):
            put_both(s2h, s2l, i, j, column[span(i - j)])
    for j in range(tiles):
        column = product(sh, sl, s2h, s2l, j)
        for i in range(j, tiles):
            block = column[span(i - j)]
            put_both(s3h, s3l, i, j, block)
            put_both(qh, ql, i, j, block - 1.25 * s2[span(i), span(j)])

    stores = []

    def store(source, target, where):
        k = len(stores)
        stores.append(pltpu.make_async_copy(source.at[where], target.at[where], out_sems.at[k]))
        stores[-1].start()

    offset = len(lower_blocks(tiles))
    last = (offset + tiles // 2) * TILE
    for j in range(tiles):
        column = product(s3h, s3l, qh, ql, j)
        for i in range(j, tiles):
            block = column[span(i - j)] + 1.25 * step_block(i, j)
            put_both(xh, xl, i, j, block)
            if i != j:
                pack[span(lower_blocks(tiles).index((i, j)))] = block
            else:
                s2[span(i), span(i)] = block
        if j + 1 < tiles:
            first = lower_blocks(tiles).index((j + 1, j))
            store(pack, pack_hbm, slice(first * TILE, (first + tiles - 1 - j) * TILE))
        if j % 2:
            first, second = s2[span(j - 1), span(j - 1)], s2[span(j), span(j)]
            pack[span(offset + j // 2)] = jnp.where(rows >= cols, first, second)
            line = jnp.sum(jnp.where(on_diag, second, 0.0), axis=0, keepdims=True)
            start = last + j // 2 * 8
            pack[start : start + 8] = jnp.broadcast_to(line, (8, TILE))
            store(pack, pack_hbm, span(offset + j // 2))
            store(pack, pack_hbm, slice(start, start + 8))
        store(xh, xh_hbm, span(j))
        store(xl, xl_hbm, span(j))
    for copy in stores:
        copy.wait()


def packed_rows(size):
    tiles = size // TILE
    return (len(lower_blocks(tiles)) + tiles // 2) * TILE + 8 * (tiles // 2)


def root(factor):
    size = factor.shape[0]
    tiles = size // TILE
    half = pltpu.HBM((size, size), jnp.bfloat16)
    square = pltpu.VMEM((size, size), jnp.float32)
    square_half = pltpu.VMEM((size, size), jnp.bfloat16)
    packed = (packed_rows(size), TILE)
    return pl.pallas_call(
        root_kernel,
        out_shape=[half, half, pltpu.HBM(packed, jnp.float32)],
        in_specs=[anywhere()],
        out_specs=[anywhere()] * 3,
        scratch_shapes=[square, square_half, square_half, square]
        + [square_half] * 8
        + [
            pltpu.VMEM(packed, jnp.float32),
            pltpu.SemaphoreType.DMA((tiles,)),
            pltpu.SemaphoreType.DMA((4 * tiles - 1,)),
        ],
        compiler_params=pltpu.CompilerParams(vmem_limit_bytes=44 * MIB),
        cost_estimate=pl.CostEstimate(flops=0, bytes_accessed=0, transcendentals=0),
        name="root",
    )(in_hbm(factor))


def unpack_block(pack_ref, tiles, i, j, rows, cols):
    if i != j:
        return pack_ref[span(lower_blocks(tiles).index((i, j)))]
    offset = len(lower_blocks(tiles))
    last = (offset + tiles // 2) * TILE
    both = pack_ref[span(offset + i // 2)]
    if i % 2 == 0:
        return jnp.where(rows >= cols, both, both.T)
    diagonal = pack_ref[last + (i // 2) * 8 : last + (i // 2) * 8 + 1]
    return jnp.where(rows == cols, diagonal, jnp.where(rows < cols, both, both.T))


def split_kernel(x_ref, high_ref, low_ref, sum_ref):
    half, size = x_ref.shape
    total = jnp.zeros((8, TILE), jnp.float32)
    for r in range(half // TILE):
        for c in range(size // TILE):
            block = x_ref[span(r), span(c)]
            put_split(high_ref, low_ref, r, c, block)
            total += jnp.sum((block * block).reshape(TILE // 8, 8, TILE), axis=0)
    sum_ref[...] = jnp.full(sum_ref.shape, jnp.sum(total), jnp.float32)


def split_rows(x):
    half = pltpu.HBM(x.shape, jnp.bfloat16)
    return pl.pallas_call(
        split_kernel,
        out_shape=[half, half, jax.ShapeDtypeStruct((8, 128), jnp.float32)],
        in_specs=[vmem()],
        out_specs=[vmem()] * 3,
        compiler_params=pltpu.CompilerParams(vmem_limit_bytes=56 * MIB),
        cost_estimate=pl.CostEstimate(flops=0, bytes_accessed=4 * 2**20, transcendentals=0),
        name="split_rows",
    )(in_hbm(x))


def raw_kernel(
    place_ref, near_sum_ref, xh_hbm, xl_hbm, pack, nh_hbm, nl_hbm, far, raw, sums_ref,
    xh, xl, nh, nl, ph, pw, fh, fl, lh, ll, uh, ul, sems,
):
    half, size = far.shape
    tiles = size // TILE
    split_at = half // TILE
    side = place_ref[0]
    rows, cols = diag_mask()
    sources, targets = (nh_hbm, nl_hbm, xh_hbm, xl_hbm), (nh, nl, xh, xl)
    loads = [
        pltpu.make_async_copy(source, target, sems.at[k])
        for k, (source, target) in enumerate(zip(sources, targets))
    ]
    for load in loads:
        load.start()

    def own_arrived():
        for load in loads[2:]:
            load.wait()

    for i in range(tiles):
        for j in range(i + 1):
            put_both(ph, pw, i, j, unpack_block(pack, tiles, i, j, rows, cols))

    def place_left(high_ref, low_ref):
        for r in range(split_at):
            source_rows = pl.ds(pl.multiple_of(place_ref[1 + r] * TILE, TILE), TILE)
            for c in range(tiles):
                source_cols = pl.ds(pl.multiple_of(place_ref[1 + c] * TILE, TILE), TILE)
                lh[c // split_at, span(r), span(c % split_at)] = high_ref[source_rows, source_cols]
                ll[c // split_at, span(r), span(c % split_at)] = low_ref[source_rows, source_cols]

    @pl.when(side == 0)
    def _():
        own_arrived()
        place_left(xh, xl)

    @pl.when(side != 0)
    def _():
        place_left(ph, pw)

    for load in loads[:2]:
        load.wait()

    total = jnp.zeros((8, TILE), jnp.float32)
    for j in range(tiles):
        block = far[:, span(j)]
        fh[:, span(j)], fl[:, span(j)] = split(block)
        total += jnp.sum((block * block).reshape(half // 8, 8, TILE), axis=0)
        column = dot3(lh[0], ll[0], nh[:, span(j)], nl[:, span(j)])
        column += dot3(lh[1], ll[1], fh[:, span(j)], fl[:, span(j)])
        uh[:, span(j)], ul[:, span(j)] = split(column)
    grad_sum = jnp.sum(total) + near_sum_ref[0, 0]

    def times_right(high_ref, low_ref):
        total = jnp.zeros((8, TILE), jnp.float32)
        for j in range(tiles):
            column = dot3(uh[...], ul[...], high_ref[:, span(j)], low_ref[:, span(j)])
            raw[:, span(j)] = column
            total += jnp.sum((column * column).reshape(half // 8, 8, TILE), axis=0)
        lane = lax.broadcasted_iota(jnp.int32, (8, 128), 1)
        sums_ref[...] = jnp.where(lane == 0, jnp.sum(total), grad_sum)

    @pl.when(side == 0)
    def _():
        times_right(ph, pw)

    @pl.when(side != 0)
    def _():
        own_arrived()
        times_right(xh, xl)


def raw_rows(place, near_sum, x_high, x_low, pack, near_high, near_low, far):
    half, size = far.shape
    wide = pltpu.VMEM((half, size), jnp.bfloat16)
    big = pltpu.VMEM((size, size), jnp.bfloat16)
    two = pltpu.VMEM((2, half, half), jnp.bfloat16)
    return pl.pallas_call(
        raw_kernel,
        out_shape=[
            pltpu.VMEM((half, size), jnp.float32),
            jax.ShapeDtypeStruct((8, 128), jnp.float32),
        ],
        in_specs=[smem(), vmem(), anywhere(), anywhere(), vmem(), anywhere(), anywhere(), vmem()],
        out_specs=[vmem(), vmem()],
        scratch_shapes=[
            big, big, wide, wide, big, big, wide, wide, two, two, wide, wide,
            pltpu.SemaphoreType.DMA((4,)),
        ],
        compiler_params=pltpu.CompilerParams(vmem_limit_bytes=40 * MIB),
        cost_estimate=pl.CostEstimate(
            flops=6 * size**3, bytes_accessed=12 * 2**20, transcendentals=0
        ),
        name="raw_rows",
    )(
        place, near_sum, in_hbm(x_high), in_hbm(x_low), resident(pack),
        in_hbm(near_high), in_hbm(near_low), resident(far),
    )


def graft_kernel(own_ref, other_ref, raw, out_hbm, buffer, sems):
    half, size = buffer.shape
    steps = sems.shape[0]
    count = size * size
    own = own_ref[...]
    raw_sum = own[:1, :1] + other_ref[:1, :1]
    grad_sum = own[:1, 1:2]
    scale = jnp.sqrt(grad_sum / count + epsilon) / jnp.sqrt(raw_sum / count + epsilon)
    stores = []
    for k in range(steps):
        rows = slice(k * half // steps, (k + 1) * half // steps)
        buffer[rows] = raw[rows] * scale
        stores.append(pltpu.make_async_copy(buffer.at[rows], out_hbm.at[rows], sems.at[k]))
        stores[-1].start()
    for store in stores:
        store.wait()


def graft(own_sums, other_sums, raw):
    steps = 4
    return pl.pallas_call(
        graft_kernel,
        out_shape=pltpu.HBM(raw.shape, jnp.float32),
        in_specs=[vmem(), vmem(), vmem()],
        out_specs=anywhere(),
        scratch_shapes=[
            pltpu.VMEM(raw.shape, jnp.float32),
            pltpu.SemaphoreType.DMA((steps,)),
        ],
        compiler_params=pltpu.CompilerParams(vmem_limit_bytes=6 * MIB),
        cost_estimate=pl.CostEstimate(flops=0, bytes_accessed=4 * 2**20, transcendentals=0),
        name="graft",
    )(own_sums, other_sums, resident(raw))


def renew_kernel(
    place_ref, a_ref, nh_ref, nl_ref, far_ref, out_ref, gh, gl, th, tl
):
    size = a_ref.shape[0]
    half = size // 2
    tiles = size // TILE
    side = place_ref[0]
    used = place_ref[1 + tiles] != 0

    for p in range(tiles):
        for c in range(tiles):
            if p < half // TILE:
                high, low = nh_ref[span(p), span(c)], nl_ref[span(p), span(c)]
            else:
                high, low = split(far_ref[span(p - half // TILE), span(c)])
            for block, target, flipped in ((high, gh, th), (low, gl, tl)):
                target[span(p), span(c)] = block
                flipped[span(c), span(p)] = block.T

    def write(i, j, block):
        rows = pl.ds(pl.multiple_of(i * TILE, TILE), TILE)
        cols = pl.ds(pl.multiple_of(j * TILE, TILE), TILE)
        gain = jnp.where(used, block * ((1.0 - decay_rate) / size), 0.0)
        out_ref[rows, cols] = decay_rate * a_ref[rows, cols] + gain

    def products(lh, ll, rh, rl, where):
        for j in range(tiles):
            low_rows = slice(j * TILE, size)
            column = dot3(lh[low_rows, :], ll[low_rows, :], rh[:, span(j)], rl[:, span(j)])
            for i in range(j, tiles):
                block = column[span(i - j)]
                write(where(i), where(j), block)
                if i != j:
                    write(where(j), where(i), block.T)

    @pl.when(side == 0)
    def _():
        products(gh, gl, th, tl, lambda i: place_ref[1 + i])

    @pl.when(side != 0)
    def _():
        products(th, tl, gh, gl, lambda i: i)


def renew(place, factor, near_high, near_low, far):
    size = factor.shape[0]
    return pl.pallas_call(
        renew_kernel,
        out_shape=jax.ShapeDtypeStruct((size, size), jnp.float32),
        in_specs=[smem()] + [vmem()] * 4,
        out_specs=vmem(),
        scratch_shapes=[pltpu.VMEM((size, size), jnp.bfloat16)] * 4,
        compiler_params=pltpu.CompilerParams(vmem_limit_bytes=56 * MIB),
        cost_estimate=pl.CostEstimate(
            flops=4 * size**3, bytes_accessed=12 * 2**20, transcendentals=0
        ),
        name="renew",
    )(place, factor, near_high, near_low, far)


def per_device(grad, factors, owners):
    row_count = grad.shape[0]
    block_size = factors.shape[-1]
    owner_count = lax.axis_size("block")
    dp_index = lax.axis_index("dp")
    blk_index = lax.axis_index("block")
    side = dp_index % 2
    slot = dp_index // 2
    outer_pair = (dp_index == 0) | (dp_index == 3)
    groups = [
        [x * owner_count + b for x in pair for b in range(owner_count)] for pair in ((0, 3), (1, 2))
    ]

    def exchange(x):
        return lax.all_to_all(
            x, BOTH, split_axis=0, concat_axis=0, tiled=True, axis_index_groups=groups
        )

    def swap(x):
        return lax.ppermute(x, "dp", [(i, i ^ 1) for i in range(4)])

    order = jnp.where(outer_pair, jnp.array([0, 3, 1, 2]), jnp.array([1, 2, 0, 3]))
    used = jnp.sum(owners == blk_index) > slot
    place = jnp.concatenate([side[None], order, used[None]]).astype(jnp.int32)

    near = exchange(deal(owners, grad, owner_count, False)).reshape(block_size // 2, block_size)
    other_grad = swap(grad)
    own_factor = factors[0, 0]
    x_high, x_low, pack = root(own_factor)
    other_pack = swap(pack)
    dealt = deal(owners, other_grad, owner_count, True)
    near, dealt = lax.optimization_barrier((near, dealt))
    far = exchange(dealt).reshape(block_size // 2, block_size)

    near_high, near_low, near_sum = split_rows(near)
    raw, sums = raw_rows(place, near_sum, x_high, x_low, other_pack, near_high, near_low, far)
    scaled = graft(sums, swap(sums), raw)
    scaled, far = lax.optimization_barrier((scaled, far))
    back = exchange(scaled.reshape(2 * owner_count, row_count, block_size))
    update = collect(owners, back)
    new_own = renew(place, own_factor, near_high, near_low, far)
    return (new_own[None, None], update)


def solution(mesh):
    placed = (P(BOTH, None), P("dp", "block", None, None), P())
    return jax.shard_map(
        per_device,
        mesh=mesh,
        in_specs=placed,
        out_specs=(P("dp", "block", None, None), P(BOTH, None)),
        check_vma=False,
    )
```

time: 154 us -> 141 us (0.916)
  Pallas kernels: 62.9 us -> 52.6 us
  starting transfers between devices: 34.6 us -> 31.4 us
  waiting for transfers between devices: 49.4 us -> 52.3 us
  local copies, waits for them, and re-layouts: 3.27 us -> 1.36 us
    pallas_call x7 -> x6, Pallas kernels: 47.6 us -> 37 us  [the longest x1 16.9 us: root(): pl.pallas_call(root_kernel, out_shape=[half, half, pltpu.HBM(packed, jnp....]
    all_to_all x3, waiting for transfers between devices: 21.2 us -> 26.2 us  [exchange(): lax.all_to_all(x, BOTH, split_axis=0, concat_axis=0, tiled=True, axis_ind...]
    all_to_all x3, starting transfers between devices: 32.7 us -> 28.8 us  [exchange(): lax.all_to_all(x, BOTH, split_axis=0, concat_axis=0, tiled=True, axis_ind...]
    ppermute x3, waiting for transfers between devices: 28.2 us -> 26.1 us  [swap(): return lax.ppermute(x, 'dp', [(i, i ^ 1) for i in range(4)])]
    unnamed x14, local copies, waits for them, and re-layouts: 3.27 us -> 1.36 us
  transfers between devices with their start and end apart: 6 -> 6, of which waited for: 5 -> 5; matrix products, arithmetic and copies ran while one was open for 1% -> 1% of each run, Pallas kernels for 28% -> 27%
where the time goes in v2:
time: 141 us; the launch traced here: 140 us
  Pallas kernels  52.6 us (37%)
  waiting for transfers between devices  52.3 us (37%)
  starting transfers between devices  31.4 us (22%)
  between operations  1.63 us (1%)
    all_to_all x3, starting transfers between devices, exchange(): lax.all_to_all(x, BOTH, split_axis=0, concat_axis=0, tiled=True, axis_ind...  28.8 us
    all_to_all x3, waiting for transfers between devices, exchange(): lax.all_to_all(x, BOTH, split_axis=0, concat_axis=0, tiled=True, axis_ind...  26.2 us
    ppermute x3, waiting for transfers between devices, swap(): return lax.ppermute(x, 'dp', [(i, i ^ 1) for i in range(4)])  26.1 us
    pallas_call x1, Pallas kernels, root(): pl.pallas_call(root_kernel, out_shape=[half, half, pltpu.HBM(packed, jnp....  16.9 us
    pallas_call x1, Pallas kernels, renew(): pl.pallas_call(renew_kernel, out_shape=jax.ShapeDtypeStruct((size, size),...  12 us
    pallas_call x1, Pallas kernels, raw_rows(): pl.pallas_call(raw_kernel, out_shape=[pltpu.VMEM((half, size), jnp.float3...  11.9 us
    pallas_call x2, Pallas kernels, deal(): pl.pallas_call(deal_resident_kernel if landed else deal_kernel, out_shape...  4.75 us
    pallas_call x1, Pallas kernels, split_rows(): pl.pallas_call(split_kernel, out_shape=[half, half, jax.ShapeDtypeStruct(...  3.6 us
  transfers between devices with their start and end apart: 6, of which 5 were waited for; matrix products, arithmetic and copies ran while one was open for 1% of the time, Pallas kernels for 27%

profile of v2, /device:TPU:1, one launch (start us, length us, event | category | flops | bytes accessed | tf_op | source)
XLA Modules:
  0.0 140.0 jit_solution(8917939895664651863)
XLA Ops:
  0.6 2.1 %collective-permute-start = (f32[8,28672]{1,0:T(8,128)}, f32[8,28672]{1,0:T(8,128)S(1)}, u32[]{:S(2)}, u32[]{:S(2)}) collective-permute-start(f32[8,28672]{1,0:T(8,128)} %grad.1), channel_id=1, source_target_pairs={{0,32},{32,0},{64,96},{96,64},{1,33},{33,1},{65,97},{97,65},{2,34}... | collective-permute-start | bytes 2752520 | tf_op jit(solution)/shard_map/ppermute | solution.py:540
  2.7 0.0 copy-start.1
  2.8 0.7 copy-done.1
  3.4 2.8 %deal.2 = f32[64,8,1024]{2,1,0:T(8,128)} custom-call(s32[28]{0:T(128)S(1)} %copy-done.1, f32[8,28672]{1,0:T(8,128)} %grad.1), custom_call_target="tpu_custom_call" | custom-call | flops 49999998976 | bytes 4194304 | tf_op jit(solution)/shard_map/deal/pallas_call | solution.py:144
  6.2 11.2 %all-to-all-start = ((f32[64,8,1024]{2,1,0:T(8,128)}), f32[64,8,1024]{2,1,0:T(8,128)}, u32[]{:S(2)}, u32[]{:S(2)}) async-start(f32[64,8,1024]{2,1,0:T(8,128)} %deal.2), calls=%async_computation | async-start | bytes 4194304 | tf_op jit(solution)/shard_map/all_to_all | solution.py:535
  17.4 0.0 copy-start.2
  17.4 16.9 %root.1 = (bf16[1024,1024]{1,0:T(8,128)(2,1)}, bf16[1024,1024]{1,0:T(8,128)(2,1)}, f32[2064,256]{1,0:T(8,128)}) custom-call(f32[1024,1024]{1,0:T(8,128)} %bitcast.10), custom_call_target="tpu_custom_call" | custom-call | tf_op jit(solution)/shard_map/root/pallas_call | solution.py:270
  34.4 0.4 collective-permute-start.1
  34.8 0.0 collective-permute-done.grad
  34.8 0.0 copy-done.2
  34.8 2.0 %deal.3 = f32[64,8,1024]{2,1,0:T(8,128)} custom-call(s32[28]{0:T(128)S(1)} %copy-done.2, f32[8,28672]{1,0:T(8,128)S(1)} %collective-permute-done.grad), custom_call_target="tpu_custom_call" | custom-call | flops 49999998976 | bytes 4194304 | tf_op jit(solution)/shard_map/deal/pallas_call | solution.py:144
  36.7 9.4 %all-to-all-done = f32[64,8,1024]{2,1,0:T(8,128)} async-done(((f32[64,8,1024]{2,1,0:T(8,128)}), f32[64,8,1024]{2,1,0:T(8,128)}, u32[]{:S(2)}, u32[]{:S(2)}) %all-to-all-start) | async-done | bytes 2097184 | tf_op jit(solution)/shard_map/all_to_all | solution.py:535
  46.1 0.0 copy-start.5
  46.1 0.0 copy-start.6
  46.1 7.0 %all-to-all-start.1 = ((f32[64,8,1024]{2,1,0:T(8,128)}), f32[64,8,1024]{2,1,0:T(8,128)S(1)}, u32[]{:S(2)}, u32[]{:S(2)}) async-start(f32[64,8,1024]{2,1,0:T(8,128)} %deal.3), calls=%async_computation.1 | async-start | bytes 4194304 | tf_op jit(solution)/shard_map/all_to_all | solution.py:535
  53.1 0.6 fusion
  54.4 0.0 copy-done.5
  54.4 0.0 copy-done.6
  54.4 0.1 pad_add_fusion.place_ref
  54.5 0.0 copy-start.3
  54.5 3.6 %split_rows.1 = (bf16[512,1024]{1,0:T(8,128)(2,1)}, bf16[512,1024]{1,0:T(8,128)(2,1)}, f32[8,128]{1,0:T(8,128)}) custom-call(f32[512,1024]{1,0:T(8,128)} %bitcast.3.x_ref), custom_call_target="tpu_custom_call" | custom-call | bytes 4194304 | tf_op jit(solution)/shard_map/split_rows/pallas_call | solution.py:313
  58.1 23.7 %collective-permute-done.1.pack = f32[2064,256]{1,0:T(8,128)} collective-permute-done((f32[2064,256]{1,0:T(8,128)}, f32[2064,256]{1,0:T(8,128)}, u32[]{:S(2)}, u32[]{:S(2)}) %collective-permute-start.1) | collective-permute-done | bytes 2113568 | tf_op jit(solution)/shard_map/ppermute | solution.py:540
  81.8 0.1 all-to-all-done.1
  81.8 0.0 copy-start
  81.8 0.0 copy-start.4
  81.8 0.7 copy-done.4
  82.5 11.9 %raw_rows.1 = (f32[512,1024]{1,0:T(8,128)S(1)}, f32[8,128]{1,0:T(8,128)S(1)}) custom-call(s32[6]{0:T(128)S(1)} %pad_add_fusion.place_ref, f32[8,128]{1,0:T(8,128)S(1)} %copy-done.4, bf16[1024,1024]{1,0:T(8,128)(2,1)} %get-tuple-element.18.xh_hbm, bf16[1024,1024]{1,0:T(8,128)(2,1)} %get-tuple-element.19.xl_hbm, f32[2064,256]{1,0:T(8,128)} %collective-permute-done.1.pack, ...), custom_call_target="tpu_custom_call" | custom-call | flops 6442450944 | bytes 12582912 | tf_op jit(solution)/shard_map/raw_rows/pallas_call | solution.py:403
  94.4 0.0 copy-done.3
  94.4 0.0 copy-done
  94.4 0.1 collective-permute-start.2
  94.5 2.4 %collective-permute-done.2.other_ref = f32[8,128]{1,0:T(8,128)S(1)} collective-permute-done((f32[8,128]{1,0:T(8,128)S(1)}, f32[8,128]{1,0:T(8,128)S(1)}, u32[]{:S(2)}, u32[]{:S(2)}) %collective-permute-start.2) | collective-permute-done | bytes 4128 | tf_op jit(solution)/shard_map/ppermute | solution.py:540
  97.0 1.6 %graft.1 = f32[512,1024]{1,0:T(8,128)} custom-call(f32[8,128]{1,0:T(8,128)S(1)} %get-tuple-element.22.own_ref, f32[8,128]{1,0:T(8,128)S(1)} %collective-permute-done.2.other_ref, f32[512,1024]{1,0:T(8,128)S(1)} %get-tuple-element.23.raw), custom_call_target="tpu_custom_call" | custom-call | bytes 4194304 | tf_op jit(solution)/shard_map/graft/pallas_call | solution.py:446
  98.5 10.6 %all-to-all-start.2 = ((f32[64,8,1024]{2,1,0:T(8,128)}), f32[64,8,1024]{2,1,0:T(8,128)S(1)}, u32[]{:S(2)}, u32[]{:S(2)}) async-start(f32[64,8,1024]{2,1,0:T(8,128)} %bitcast.9), calls=%async_computation.2 | async-start | bytes 4194304 | tf_op jit(solution)/shard_map/all_to_all | solution.py:535
  109.2 12.0 %renew.1 = f32[1024,1024]{1,0:T(8,128)} custom-call(s32[6]{0:T(128)} %copy-done.3, f32[1024,1024]{1,0:T(8,128)} %bitcast.11, bf16[512,1024]{1,0:T(8,128)(2,1)} %get-tuple-element.15.nh_hbm.nh_ref, bf16[512,1024]{1,0:T(8,128)(2,1)} %get-tuple-element.16.nl_hbm.nl_ref, f32[512,1024]{1,0:T(8,128)} %bitcast.8), custom_call_target="tpu_custom_call" | custom-call | flops 4294967296 | bytes 12582912 | tf_op jit(solution)/shard_map/renew/pallas_call | solution.py:507
  121.2 16.8 %all-to-all-done.2.back = f32[64,8,1024]{2,1,0:T(8,128)S(1)} async-done(((f32[64,8,1024]{2,1,0:T(8,128)}), f32[64,8,1024]{2,1,0:T(8,128)S(1)}, u32[]{:S(2)}, u32[]{:S(2)}) %all-to-all-start.2) | async-done | bytes 2097184 | tf_op jit(solution)/shard_map/all_to_all | solution.py:535
  138.0 1.9 %collect.1 = f32[8,28672]{1,0:T(8,128)} custom-call(s32[28]{0:T(128)S(1)} %copy-done.2, f32[64,8,1024]{2,1,0:T(8,128)S(1)} %all-to-all-done.2.back), custom_call_target="tpu_custom_call" | custom-call | bytes 4194304 | tf_op jit(solution)/shard_map/collect/pallas_call | solution.py:158
  (1 shorter events, 0.0 us)
Async XLA Ops:
  0.6 34.1 %collective-permute-start = (f32[8,28672]{1,0:T(8,128)}, f32[8,28672]{1,0:T(8,128)S(1)}, u32[]{:S(2)}, u32[]{:S(2)}) collective-permute-start(f32[8,28672]{1,0:T(8,128)} %grad.1), channel_id=1, source_target_pairs={{0,32},{32,0},{64,96},{96,64},{1,33},{33,1},{65,97},{97,65},{2,34}... | collective-permute-start | bytes 2752520 | tf_op jit(solution)/shard_map/ppermute | solution.py:540
  2.7 0.7 copy-start.1
  6.2 39.9 %all-to-all-start = ((f32[64,8,1024]{2,1,0:T(8,128)}), f32[64,8,1024]{2,1,0:T(8,128)}, u32[]{:S(2)}, u32[]{:S(2)}) async-start(f32[64,8,1024]{2,1,0:T(8,128)} %deal.2), calls=%async_computation | async-start | bytes 4194304 | tf_op jit(solution)/shard_map/all_to_all | solution.py:535
  17.4 17.4 %copy-start.2 = (s32[28]{0:T(128)S(1)}, s32[28]{0:T(128)}, u32[]{:S(2)}) copy-start(s32[28]{0:T(128)} %owners_ref.5) | copy-start | bytes 340
  34.4 47.4 %collective-permute-start.1 = (f32[2064,256]{1,0:T(8,128)}, f32[2064,256]{1,0:T(8,128)}, u32[]{:S(2)}, u32[]{:S(2)}) collective-permute-start(f32[2064,256]{1,0:T(8,128)} %get-tuple-element.20), channel_id=1, source_target_pairs={{0,32},{32,0},{64,96},{96,64},{1,33},{33,1},{65,97},{97,65},{2,34}... | collective-permute-start | bytes 6340616 | tf_op jit(solution)/shard_map/ppermute | solution.py:540
  46.1 8.3 %copy-start.5 = (s32[4]{0:T(128)S(1)}, s32[4]{0:T(128)}, u32[]{:S(2)}) copy-start(s32[4]{0:T(128)} %constant.41.clone) | copy-start | bytes 52
  46.1 8.3 %copy-start.6 = (s32[4]{0:T(128)S(1)}, s32[4]{0:T(128)}, u32[]{:S(2)}) copy-start(s32[4]{0:T(128)} %constant.40.clone) | copy-start | bytes 52
  46.1 35.7 %all-to-all-start.1 = ((f32[64,8,1024]{2,1,0:T(8,128)}), f32[64,8,1024]{2,1,0:T(8,128)S(1)}, u32[]{:S(2)}, u32[]{:S(2)}) async-start(f32[64,8,1024]{2,1,0:T(8,128)} %deal.3), calls=%async_computation.1 | async-start | bytes 4194304 | tf_op jit(solution)/shard_map/all_to_all | solution.py:535
  54.5 39.9 %copy-start.3 = (s32[6]{0:T(128)}, s32[6]{0:T(128)S(1)}, u32[]{:S(2)}) copy-start(s32[6]{0:T(128)S(1)} %pad_add_fusion.place_ref) | copy-start | bytes 76
  81.8 12.6 %copy-start = (f32[64,8,1024]{2,1,0:T(8,128)}, f32[64,8,1024]{2,1,0:T(8,128)S(1)}, u32[]{:S(2)}) copy-start(f32[64,8,1024]{2,1,0:T(8,128)S(1)} %all-to-all-done.1) | copy-start | bytes 6291460
  81.8 0.7 copy-start.4
  94.4 2.5 %collective-permute-start.2 = (f32[8,128]{1,0:T(8,128)S(1)}, f32[8,128]{1,0:T(8,128)S(1)}, u32[]{:S(2)}, u32[]{:S(2)}) collective-permute-start(f32[8,128]{1,0:T(8,128)S(1)} %get-tuple-element.22.own_ref), channel_id=1, source_target_pairs={{0,32},{32,0},{64,96},{96,64},{1,33},{33,1},{65,97},{97,65},{2,34}... | collective-permute-start | bytes 12296 | tf_op jit(solution)/shard_map/ppermute | solution.py:540
  98.5 39.4 %all-to-all-start.2 = ((f32[64,8,1024]{2,1,0:T(8,128)}), f32[64,8,1024]{2,1,0:T(8,128)S(1)}, u32[]{:S(2)}, u32[]{:S(2)}) async-start(f32[64,8,1024]{2,1,0:T(8,128)} %bitcast.9), calls=%async_computation.2 | async-start | bytes 4194304 | tf_op jit(solution)/shard_map/all_to_all | solution.py:535
